TPU v7x, 512 devices: a whole 4x8x8 slice. The times are simulated.
512 devices in a mesh: lat: 16 (over z_lo, y), lon: 32 (over x, z_hi, core).
Axes of the slice: x: 4, y: 8, z: 8 (z_hi: 4, z_lo: 2; z = z_hi * 2 + z_lo), core: 2. Of those that a mesh axis runs over, the one named last changes fastest.
Arguments:
- queries: bfloat16 [128, 512, 1024], P('lat', 'lon'), may hold values from -8 to 8
- keys: bfloat16 [128, 512, 1024], P('lat', 'lon'), may hold values from -8 to 8
- values: bfloat16 [128, 512, 1024], P('lat', 'lon'), may hold values from -6 to 6
- cotangent: bfloat16 [128, 512, 1024], P('lat', 'lon'), may hold values from -6 to 6
Outputs:
- attended: bfloat16 [128, 512, 1024], P('lat', 'lon')
- query_grad: bfloat16 [128, 512, 1024], P('lat', 'lon')
- key_grad: bfloat16 [128, 512, 1024], P('lat', 'lon')
- value_grad: bfloat16 [128, 512, 1024], P('lat', 'lon')
All inputs are finite; a program needn't handle non-finite values.
Results may differ from a plain program's by a relative error of at most 0.009.
Values may be sent and summed in bfloat16 or wider, within the bound.
A program may use at most 64 MiB of HBM per device.

v0:
```python
import jax
import jax.numpy as jnp
from jax import lax
from jax.sharding import PartitionSpec as P

HD = 64
REACH = 6


def padded(x, sides, width, wrap):
    for axis, dim in sides:
        peers, length = (lax.axis_size(axis), x.shape[dim])
        up = [(i, (i + 1) % peers) for i in range(peers if wrap else peers - 1)]
        down = [(j, i) for i, j in up]
        last = lax.slice_in_dim(x, length - width, length, axis=dim)
        leading = lax.slice_in_dim(x, 0, width, axis=dim)
        before = lax.ppermute(last, axis, up)
        after = lax.ppermute(leading, axis, down)
        x = jnp.concatenate([before, x, after], axis=dim)
    return x


def passed_along(x, axis, by):
    peers = lax.axis_size(axis)
    pairs = [(i, i + by) for i in range(peers) if 0 <= i + by < peers]
    return lax.ppermute(x, axis, pairs)


def from_behind(block, axis, distance):
    devices = range(lax.axis_size(axis))
    route = [((i - distance) % len(devices), i) for i in devices]
    return lax.ppermute(block, axis, route)


def window_mask(inner, outer, cols, reach):
    inner_row = jnp.repeat(jnp.arange(inner), cols)
    inner_col = jnp.tile(jnp.arange(cols), inner)
    outer_cols = cols + 2 * reach
    outer_row = jnp.repeat(jnp.arange(outer), outer_cols)
    outer_col = jnp.tile(jnp.arange(outer_cols), outer)
    row_gap = outer_row[None, :] - inner_row[:, None]
    col_gap = outer_col[None, :] - inner_col[:, None]
    near = (row_gap >= 0) & (row_gap <= 2 * reach) & (col_gap >= 0) & (col_gap <= 2 * reach)
    return (near, outer_row)


def body(queries, keys, values, cotangent):
    rows, cols, width = queries.shape
    heads = width // HD
    scale = HD ** (-0.5)
    block = 8
    outer = block + 2 * REACH
    outer_cols = cols + 2 * REACH
    first_row = lax.axis_index("lat") * rows
    total_rows = rows * lax.axis_size("lat")
    near, outer_row = window_mask(block, outer, cols, REACH)
    stacked = jnp.stack((keys, values))
    banded = padded(stacked, (("lat", 1),), REACH, False)
    rimmed = padded(banded, (("lon", 2),), REACH, True)
    key_lat = first_row + 0 + outer_row - REACH
    mask = near & ((key_lat >= 0) & (key_lat < total_rows))[None, :]
    query_block = queries.reshape(block * cols, heads, HD)
    upstream = cotangent.reshape(block * cols, heads, HD)
    rim_block = rimmed.reshape(2, outer * outer_cols, heads, HD)
    scores = (
        jnp.einsum("qhd,khd->hqk", query_block, rim_block[0], preferred_element_type=jnp.float32)
        * scale
    )
    peak = jnp.max(jnp.where(mask, scores, -1e30), axis=-1, keepdims=True)
    summed = jnp.sum(jnp.where(mask, jnp.exp(scores - peak), 0.0), axis=-1, keepdims=True)
    log_total = peak + jnp.log(summed)
    probs = jnp.where(mask, jnp.exp(scores - log_total), 0.0)
    probs_low = probs.astype(jnp.bfloat16)
    attended_parts = jnp.einsum(
        "hqk,khd->qhd", probs_low, rim_block[1], preferred_element_type=jnp.float32
    ).astype(jnp.bfloat16)
    prob_grad = jnp.einsum(
        "qhd,khd->hqk", upstream, rim_block[1], preferred_element_type=jnp.float32
    )
    delta = jnp.sum(probs * prob_grad, axis=-1, keepdims=True)
    score_grad = (probs * (prob_grad - delta)).astype(jnp.bfloat16)
    query_parts = (
        scale
        * jnp.einsum("hqk,khd->qhd", score_grad, rim_block[0], preferred_element_type=jnp.float32)
    ).astype(jnp.bfloat16)
    stat_parts = jnp.concatenate((log_total[:, :, 0], delta[:, :, 0]), axis=0).T
    key_part = scale * jnp.einsum(
        "hqk,qhd->khd", score_grad, query_block, preferred_element_type=jnp.float32
    )
    value_part = jnp.einsum("hqk,qhd->khd", probs_low, upstream, preferred_element_type=jnp.float32)
    grad_parts = jnp.stack((key_part, value_part)).reshape(2, outer, outer_cols, width)
    attended = attended_parts.reshape(rows, cols, width)
    query_grad = query_parts.reshape(rows, cols, width)
    stats = stat_parts.reshape(rows, cols, 2 * heads)
    grads = grad_parts
    attended, query_grad, stats, grads = (attended, query_grad, stats, grads)
    from_below = passed_along(grads[:, :REACH].astype(jnp.bfloat16), "lat", -1).astype(jnp.float32)
    from_above = passed_along(grads[:, rows + REACH :].astype(jnp.bfloat16), "lat", 1).astype(
        jnp.float32
    )
    middle = grads[:, REACH : rows + REACH]
    middle = middle.at[:, rows - REACH :].add(from_below).at[:, :REACH].add(from_above)
    from_east = from_behind(middle[:, :, :REACH].astype(jnp.bfloat16), "lon", -1).astype(
        jnp.float32
    )
    from_west = from_behind(middle[:, :, cols + REACH :].astype(jnp.bfloat16), "lon", 1).astype(
        jnp.float32
    )
    inside = middle[:, :, REACH : cols + REACH]
    inside = inside.at[:, :, cols - REACH :].add(from_east).at[:, :, :REACH].add(from_west)
    key_grad = inside[0].astype(jnp.bfloat16)
    value_grad = inside[1].astype(jnp.bfloat16)
    return (attended, query_grad, key_grad, value_grad)


def solution(mesh):
    placed = (
        P("lat", "lon", None),
        P("lat", "lon", None),
        P("lat", "lon", None),
        P("lat", "lon", None),
    )
    return jax.shard_map(
        body,
        mesh=mesh,
        in_specs=placed,
        out_specs=(
            P("lat", "lon", None),
            P("lat", "lon", None),
            P("lat", "lon", None),
            P("lat", "lon", None),
        ),
        check_vma=False,
    )
```

profile of v0, /device:TPU:64, one launch (start us, length us, event | category | flops | bytes accessed | tf_op | source)
XLA Modules:
  0.0 167.8 jit_solution(3407198840886220082)
XLA Ops:
  1.9 4.5 %collective-permute-start.1 = (bf16[2,6,16,1024]{3,2,1,0:T(8,128)(2,1)S(1)}, bf16[2,6,16,1024]{3,2,1,0:T(8,128)(2,1)S(1)}, u32[]{:S(2)}, u32[]{:S(2)}) collective-permute-start(bf16[2,6,16,1024]{3,2,1,0:T(8,128)(2,1)S(1)} %get-tuple-element.67), channel_id=1, source_target_pairs={{32,0},{64,32},{96,64},{128,96},{160,128},{192,160},{224,192},{256... | collective-permute-start | bytes 1179656 | tf_op jit(solution)/shard_map/ppermute | solution.py:18
  8.3 6.4 %collective-permute-done.1 = bf16[2,6,16,1024]{3,2,1,0:T(8,128)(2,1)S(1)} collective-permute-done((bf16[2,6,16,1024]{3,2,1,0:T(8,128)(2,1)S(1)}, bf16[2,6,16,1024]{3,2,1,0:T(8,128)(2,1)S(1)}, u32[]{:S(2)}, u32[]{:S(2)}) %collective-permute-start.1) | collective-permute-done | bytes 393248 | tf_op jit(solution)/shard_map/ppermute | solution.py:18
  14.8 6.2 %collective-permute-done = bf16[2,6,16,1024]{3,2,1,0:T(8,128)(2,1)S(1)} collective-permute-done((bf16[2,6,16,1024]{3,2,1,0:T(8,128)(2,1)S(1)}, bf16[2,6,16,1024]{3,2,1,0:T(8,128)(2,1)S(1)}, u32[]{:S(2)}, u32[]{:S(2)}) %collective-permute-start) | collective-permute-done | bytes 393248 | tf_op jit(solution)/shard_map/ppermute | solution.py:17
  22.9 11.4 %collective-permute-start.3 = (bf16[2,20,6,1024]{3,0,2,1:T(2,128)(2,1)S(1)}, bf16[2,20,6,1024]{3,0,2,1:T(2,128)(2,1)}, u32[]{:S(2)}, u32[]{:S(2)}) collective-permute-start(bf16[2,20,6,1024]{3,0,2,1:T(2,128)(2,1)S(1)} %copy.47), channel_id=1, source_target_pairs={{1,0},{2,1},{3,2},{4,3},{5,4},{6,5},{7,6},{8,7},{9,8},{10,9},{11,1... | collective-permute-start | bytes 1474568 | tf_op jit(solution)/shard_map/ppermute | solution.py:18
  41.8 9.7 %collective-permute-done.2 = bf16[2,20,6,1024]{3,0,2,1:T(2,128)(2,1)} collective-permute-done((bf16[2,20,6,1024]{3,0,2,1:T(2,128)(2,1)}, bf16[2,20,6,1024]{3,0,2,1:T(2,128)(2,1)}, u32[]{:S(2)}, u32[]{:S(2)}) %collective-permute-start.2) | collective-permute-done | bytes 491552 | tf_op jit(solution)/shard_map/ppermute | solution.py:17
  56.2 3.2 %squeeze.4 = bf16[560,16,64]{2,1,0:T(8,128)(2,1)S(1)} reshape(bf16[1,20,28,1024]{3,2,1,0:T(8,128)(2,1)} %get-tuple-element.59) | data formatting | bytes 2293760 | tf_op jit(solution)/shard_map/squeeze | solution.py:75
  59.4 3.7 %copy.52 = bf16[560,16,64]{0,2,1:T(8,128)(2,1)} copy(bf16[560,16,64]{2,1,0:T(8,128)(2,1)S(1)} %squeeze.4) | data formatting | bytes 2293760 | tf_op jit(solution)/shard_map/squeeze | solution.py:75
  63.1 4.2 %squeeze.5 = bf16[560,16,64]{2,1,0:T(8,128)(2,1)} reshape(bf16[1,20,28,1024]{3,2,1,0:T(8,128)(2,1)} %get-tuple-element.58) | data formatting | bytes 2293760 | tf_op jit(solution)/shard_map/squeeze | solution.py:66
  67.3 3.8 %copy.50 = bf16[560,16,64]{0,2,1:T(8,128)(2,1)S(1)} copy(bf16[560,16,64]{2,1,0:T(8,128)(2,1)} %squeeze.5) | data formatting | bytes 2293760 | tf_op jit(solution)/shard_map/squeeze | solution.py:66
  73.2 2.5 %convolution_bitcast_fusion = f32[560,16,64]{0,2,1:T(8,128)} fusion(bf16[128,16,64]{0,2,1:T(8,128)(2,1)S(1)} %copy.55, f32[16,560,128]{2,1,0:T(8,128)S(1)} %get-tuple-element.69, f32[16,128]{1,0:T(8,128)S(1)} %log_add_fusion, pred[128,560]{0,1:T(8,128)(4,1)S(1)} %fusion.19), kind=kOutput, calls=%fused_computation.17 | convolution fusion | flops 151388160 | bytes 7223296 | tf_op jit(solution)/shard_map/hqk,qhd->khd/dot_general | solution.py:90
  80.2 2.4 %multiply_bitcast_fusion = f32[560,16,64]{0,2,1:T(8,128)} fusion(bf16[16,128,560]{1,2,0:T(8,128)(2,1)S(1)} %fusion.2, bf16[128,16,64]{0,2,1:T(8,128)(2,1)S(1)} %copy.51), kind=kOutput, calls=%fused_computation.15 | convolution fusion | flops 147374080 | bytes 4849664 | tf_op jit(solution)/shard_map/hqk,qhd->khd/dot_general | solution.py:87
  82.6 5.7 %copy.59 = f32[560,16,64]{2,1,0:T(8,128)} copy(f32[560,16,64]{0,2,1:T(8,128)} %multiply_bitcast_fusion) | data formatting | bytes 4587520 | tf_op jit(solution)/shard_map/mul | solution.py:87
  88.3 5.1 %stack.21 = f32[1,20,28,1024]{3,2,1,0:T(8,128)} reshape(f32[560,16,64]{2,1,0:T(8,128)} %copy.59) | data formatting | bytes 4587520 | tf_op jit(solution)/shard_map/stack | solution.py:91
  93.4 3.6 %constant_dynamic-update-slice_fusion.1 = f32[2,20,28,1024]{3,2,1,0:T(8,128)} fusion(f32[1,20,28,1024]{3,2,1,0:T(8,128)} %stack.21), kind=kLoop, calls=%fused_computation.46 | loop fusion | bytes 4915200
  96.9 5.7 %copy.61 = f32[560,16,64]{2,1,0:T(8,128)} copy(f32[560,16,64]{0,2,1:T(8,128)} %convolution_bitcast_fusion) | data formatting | bytes 4587520 | tf_op jit(solution)/shard_map/hqk,qhd->khd/transpose | solution.py:90
  102.6 5.1 %stack.22 = f32[1,20,28,1024]{3,2,1,0:T(8,128)} reshape(f32[560,16,64]{2,1,0:T(8,128)} %copy.61) | data formatting | bytes 4587520 | tf_op jit(solution)/shard_map/stack | solution.py:91
  107.7 3.6 %constant_dynamic-update-slice_fusion = f32[2,20,28,1024]{3,2,1,0:T(8,128)} fusion(f32[2,20,28,1024]{3,2,1,0:T(8,128)} %constant_dynamic-update-slice_fusion.1, f32[1,20,28,1024]{3,2,1,0:T(8,128)} %stack.22), kind=kLoop, calls=%fused_computation.45 | loop fusion | bytes 5242880 | tf_op jit(solution)/shard_map/stack | solution.py:91
  111.3 2.9 %convert.12 = bf16[2,20,28,1024]{3,2,1,0:T(8,128)(2,1)S(1)} convert(f32[2,20,28,1024]{3,2,1,0:T(8,128)} %constant_dynamic-update-slice_fusion) | non-fusion elementwise | flops 1146880 | bytes 6881280 | tf_op jit(solution)/shard_map/convert.5
  116.0 5.1 %collective-permute-start.4 = (bf16[2,6,28,1024]{3,0,2,1:T(2,128)(2,1)}, bf16[2,6,28,1024]{3,0,2,1:T(2,128)(2,1)}, u32[]{:S(2)}, u32[]{:S(2)}) collective-permute-start(bf16[2,6,28,1024]{3,0,2,1:T(2,128)(2,1)} %copy.62), channel_id=1, source_target_pairs={{32,0},{64,32},{96,64},{128,96},{160,128},{192,160},{224,192},{256... | collective-permute-start | bytes 2064392 | tf_op jit(solution)/shard_map/ppermute | solution.py:26
  128.2 2.2 %copy.53 = bf16[128,16,64]{2,1,0:T(8,128)(2,1)} copy(bf16[128,16,64]{0,2,1:T(8,128)(2,1)} %fusion.13) | data formatting | bytes 524288 | tf_op jit(solution)/shard_map/convert_element_type | solution.py:76
  134.4 5.2 %collective-permute-done.5 = bf16[2,6,28,1024]{3,0,2,1:T(2,128)(2,1)} collective-permute-done((bf16[2,6,28,1024]{3,0,2,1:T(2,128)(2,1)}, bf16[2,6,28,1024]{3,0,2,1:T(2,128)(2,1)}, u32[]{:S(2)}, u32[]{:S(2)}) %collective-permute-start.5) | collective-permute-done | bytes 688160 | tf_op jit(solution)/shard_map/ppermute | solution.py:26
  142.2 6.8 %collective-permute-start.6 = (bf16[2,8,6,1024]{3,2,1,0:T(8,128)(2,1)}, bf16[2,8,6,1024]{3,2,1,0:T(8,128)(2,1)}, u32[]{:S(2)}, u32[]{:S(2)}) collective-permute-start(bf16[2,8,6,1024]{3,2,1,0:T(8,128)(2,1)} %get-tuple-element.63), channel_id=1, source_target_pairs={{1,0},{2,1},{3,2},{4,3},{5,4},{6,5},{7,6},{8,7},{9,8},{10,9},{11,1... | collective-permute-start | bytes 589832 | tf_op jit(solution)/shard_map/ppermute | solution.py:32
  156.8 2.3 %scatter-add.16 = f32[2,8,16,1024]{3,2,1,0:T(8,128)S(1)} dynamic-update-slice(f32[2,8,16,1024]{3,2,1,0:T(8,128)S(1)} %slice.199, f32[2,8,6,1024]{3,2,1,0:T(8,128)} %slice_add_fusion.3, s32[]{:T(128)} %constant.122.clone.1, s32[]{:T(128)} %constant.122.clone.1, s32[]{:T(128)} %constant.134.clone.1, s32[]{:T(128)} %constant.122.clone.1) | dynamic-update-slice | bytes 786436 | tf_op jit(solution)/shard_map/scatter-add | solution.py:110
  159.1 5.9 %collective-permute-done.7 = bf16[2,8,6,1024]{3,2,1,0:T(8,128)(2,1)} collective-permute-done((bf16[2,8,6,1024]{3,2,1,0:T(8,128)(2,1)S(1)}, bf16[2,8,6,1024]{3,2,1,0:T(8,128)(2,1)}, u32[]{:S(2)}, u32[]{:S(2)}) %collective-permute-start.7) | collective-permute-done | bytes 196640 | tf_op jit(solution)/shard_map/ppermute | solution.py:32
  (79 shorter events, 49.3 us)
Async XLA Ops:
  1.9 12.8 %collective-permute-start.1 = (bf16[2,6,16,1024]{3,2,1,0:T(8,128)(2,1)S(1)}, bf16[2,6,16,1024]{3,2,1,0:T(8,128)(2,1)S(1)}, u32[]{:S(2)}, u32[]{:S(2)}) collective-permute-start(bf16[2,6,16,1024]{3,2,1,0:T(8,128)(2,1)S(1)} %get-tuple-element.67), channel_id=1, source_target_pairs={{32,0},{64,32},{96,64},{128,96},{160,128},{192,160},{224,192},{256... | collective-permute-start | bytes 1179656 | tf_op jit(solution)/shard_map/ppermute | solution.py:18
  6.4 14.6 %collective-permute-start = (bf16[2,6,16,1024]{3,2,1,0:T(8,128)(2,1)S(1)}, bf16[2,6,16,1024]{3,2,1,0:T(8,128)(2,1)S(1)}, u32[]{:S(2)}, u32[]{:S(2)}) collective-permute-start(bf16[2,6,16,1024]{3,2,1,0:T(8,128)(2,1)S(1)} %get-tuple-element.66), channel_id=1, source_target_pairs={{0,32},{32,64},{64,96},{96,128},{128,160},{160,192},{192,224},{224... | collective-permute-start | bytes 1179656 | tf_op jit(solution)/shard_map/ppermute | solution.py:17
  22.2 15.8 %copy-start.7 = (bf16[8,16,1024]{2,1,0:T(8,128)(2,1)S(1)}, bf16[8,16,1024]{2,1,0:T(8,128)(2,1)}, u32[]{:S(2)}) copy-start(bf16[8,16,1024]{2,1,0:T(8,128)(2,1)} %param.12) | copy-start | bytes 786436
  22.4 16.4 %copy-start.8 = (bf16[8,16,1024]{2,1,0:T(8,128)(2,1)S(1)}, bf16[8,16,1024]{2,1,0:T(8,128)(2,1)}, u32[]{:S(2)}) copy-start(bf16[8,16,1024]{2,1,0:T(8,128)(2,1)} %param.15) | copy-start | bytes 786436
  22.9 17.7 %collective-permute-start.3 = (bf16[2,20,6,1024]{3,0,2,1:T(2,128)(2,1)S(1)}, bf16[2,20,6,1024]{3,0,2,1:T(2,128)(2,1)}, u32[]{:S(2)}, u32[]{:S(2)}) collective-permute-start(bf16[2,20,6,1024]{3,0,2,1:T(2,128)(2,1)S(1)} %copy.47), channel_id=1, source_target_pairs={{1,0},{2,1},{3,2},{4,3},{5,4},{6,5},{7,6},{8,7},{9,8},{10,9},{11,1... | collective-permute-start | bytes 1474568 | tf_op jit(solution)/shard_map/ppermute | solution.py:18
  35.6 15.9 %collective-permute-start.2 = (bf16[2,20,6,1024]{3,0,2,1:T(2,128)(2,1)}, bf16[2,20,6,1024]{3,0,2,1:T(2,128)(2,1)}, u32[]{:S(2)}, u32[]{:S(2)}) collective-permute-start(bf16[2,20,6,1024]{3,0,2,1:T(2,128)(2,1)} %copy.46), channel_id=1, source_target_pairs={{0,1},{1,2},{2,3},{3,4},{4,5},{5,6},{6,7},{7,8},{8,9},{9,10},{10,1... | collective-permute-start | bytes 1474568 | tf_op jit(solution)/shard_map/ppermute | solution.py:17
  38.0 14.8 %copy-start.5 = (bf16[8,16,1024]{2,1,0:T(8,128)(2,1)S(1)}, bf16[8,16,1024]{2,1,0:T(8,128)(2,1)}, u32[]{:S(2)}) copy-start(bf16[8,16,1024]{2,1,0:T(8,128)(2,1)} %param.13) | copy-start | bytes 786436
  38.0 14.8 %copy-start.6 = (bf16[8,16,1024]{2,1,0:T(8,128)(2,1)S(1)}, bf16[8,16,1024]{2,1,0:T(8,128)(2,1)}, u32[]{:S(2)}) copy-start(bf16[8,16,1024]{2,1,0:T(8,128)(2,1)} %param.14) | copy-start | bytes 786436
  72.3 5.2 %copy-start = (f32[16,560,128]{2,1,0:T(8,128)}, f32[16,560,128]{2,1,0:T(8,128)S(1)}, u32[]{:S(2)}) copy-start(f32[16,560,128]{2,1,0:T(8,128)S(1)} %get-tuple-element.69) | copy-start | bytes 13762564
  73.2 2.5 %copy-start.3 = (bf16[560,16,64]{0,2,1:T(8,128)(2,1)S(1)}, bf16[560,16,64]{0,2,1:T(8,128)(2,1)}, u32[]{:S(2)}) copy-start(bf16[560,16,64]{0,2,1:T(8,128)(2,1)} %copy.52) | copy-start | bytes 3440644
  78.8 1.4 copy-start.1
  111.3 15.0 %slice-start = ((s8[4587520]{0:T(1024)(128)(4,1)}), s8[393216]{0:T(1024)(128)(4,1)S(1)}, s32[]{:S(2)}) async-start(s8[4587520]{0:T(1024)(128)(4,1)} %bitcast.57), calls=%async_computation | async-start | bytes 786432
  114.3 12.1 %slice-start.1 = ((s8[4587520]{0:T(1024)(128)(4,1)}), s8[4194304]{0:T(1024)(128)(4,1)S(1)}, s32[]{:S(2)}) async-start(s8[4587520]{0:T(1024)(128)(4,1)} %bitcast.57), calls=%async_computation.1 | async-start | bytes 8388608
  116.0 10.3 %copy-start.4 = (bf16[560,16,64]{0,2,1:T(8,128)(2,1)S(1)}, bf16[560,16,64]{0,2,1:T(8,128)(2,1)}, u32[]{:S(2)}) copy-start(bf16[560,16,64]{0,2,1:T(8,128)(2,1)} %copy.52) | copy-start | bytes 3440644
  116.0 16.5 %collective-permute-start.4 = (bf16[2,6,28,1024]{3,0,2,1:T(2,128)(2,1)}, bf16[2,6,28,1024]{3,0,2,1:T(2,128)(2,1)}, u32[]{:S(2)}, u32[]{:S(2)}) collective-permute-start(bf16[2,6,28,1024]{3,0,2,1:T(2,128)(2,1)} %copy.62), channel_id=1, source_target_pairs={{32,0},{64,32},{96,64},{128,96},{160,128},{192,160},{224,192},{256... | collective-permute-start | bytes 2064392 | tf_op jit(solution)/shard_map/ppermute | solution.py:26
  124.4 15.2 %collective-permute-start.5 = (bf16[2,6,28,1024]{3,0,2,1:T(2,128)(2,1)}, bf16[2,6,28,1024]{3,0,2,1:T(2,128)(2,1)}, u32[]{:S(2)}, u32[]{:S(2)}) collective-permute-start(bf16[2,6,28,1024]{3,0,2,1:T(2,128)(2,1)} %copy.64), channel_id=1, source_target_pairs={{0,32},{32,64},{64,96},{96,128},{128,160},{160,192},{192,224},{224... | collective-permute-start | bytes 2064392 | tf_op jit(solution)/shard_map/ppermute | solution.py:26
  141.2 7.8 %copy-start.2 = (bf16[16,128,560]{1,2,0:T(8,128)(2,1)S(1)}, bf16[16,128,560]{1,2,0:T(8,128)(2,1)}, u32[]{:S(2)}) copy-start(bf16[16,128,560]{1,2,0:T(8,128)(2,1)} %copy-done.1) | copy-start | bytes 6881284
  142.2 12.8 %collective-permute-start.6 = (bf16[2,8,6,1024]{3,2,1,0:T(8,128)(2,1)}, bf16[2,8,6,1024]{3,2,1,0:T(8,128)(2,1)}, u32[]{:S(2)}, u32[]{:S(2)}) collective-permute-start(bf16[2,8,6,1024]{3,2,1,0:T(8,128)(2,1)} %get-tuple-element.63), channel_id=1, source_target_pairs={{1,0},{2,1},{3,2},{4,3},{5,4},{6,5},{7,6},{8,7},{9,8},{10,9},{11,1... | collective-permute-start | bytes 589832 | tf_op jit(solution)/shard_map/ppermute | solution.py:32
  150.4 2.7 %copy-start.9 = (bf16[2,8,6,1024]{3,2,1,0:T(8,128)(2,1)S(1)}, bf16[2,8,6,1024]{3,2,1,0:T(8,128)(2,1)}, u32[]{:S(2)}) copy-start(bf16[2,8,6,1024]{3,2,1,0:T(8,128)(2,1)} %get-tuple-element.62) | copy-start | bytes 589828
  153.0 12.0 %collective-permute-start.7 = (bf16[2,8,6,1024]{3,2,1,0:T(8,128)(2,1)S(1)}, bf16[2,8,6,1024]{3,2,1,0:T(8,128)(2,1)}, u32[]{:S(2)}, u32[]{:S(2)}) collective-permute-start(bf16[2,8,6,1024]{3,2,1,0:T(8,128)(2,1)S(1)} %copy-done.9), channel_id=1, source_target_pairs={{31,0},{0,1},{1,2},{2,3},{3,4},{4,5},{5,6},{6,7},{7,8},{8,9},{9,10... | collective-permute-start | bytes 589832 | tf_op jit(solution)/shard_map/ppermute | solution.py:32
where the time goes:
time: 169 us; the launch traced here: 168 us
  local copies, waits for them, and re-layouts  69.9 us (41%)
  starting transfers between devices  35.4 us (21%)
  waiting for transfers between devices  34.3 us (20%)
  other arithmetic  16.1 us (10%)
  matrix products  11 us (7%)
    ppermute x2, waiting for transfers between devices, padded(): before = lax.ppermute(last, axis, up)  16 us
    ppermute x2, starting transfers between devices, padded(): after = lax.ppermute(leading, axis, down)  15.8 us
    another operation x3, local copies, waits for them, and re-layouts, body(): jnp.stack((key_part, value_part)).reshape(2, outer, outer_cols, width)  13.8 us
    ppermute x2, starting transfers between devices, from_behind(): return lax.ppermute(block, axis, route)  8.71 us
    squeeze x2, local copies, waits for them, and re-layouts, body(): rim_block[0]  8.01 us
    ppermute x2, waiting for transfers between devices, padded(): after = lax.ppermute(leading, axis, down)  7.15 us
    ppermute x2, starting transfers between devices, passed_along(): return lax.ppermute(x, axis, pairs)  6.99 us
    squeeze x2, local copies, waits for them, and re-layouts, body(): rim_block[1]  6.91 us
  transfers between devices with their start and end apart: 8, of which 6 were waited for; matrix products, arithmetic and copies ran while one was open for 14% of the time, Pallas kernels for 0%

commit v1 on v0

v1 whole, which is shorter than its diff:
```python
import functools

import jax
import jax.numpy as jnp
from jax import lax
from jax.experimental import pallas as pl
from jax.experimental.pallas import tpu as pltpu
from jax.sharding import PartitionSpec as P

HD = 64
REACH = 6
MESH = pl.DeviceIdType.MESH
BF16 = jnp.bfloat16
F32 = jnp.float32

OWN, NORTH, SOUTH, OUTER, OUTER_N, OUTER_S, INNER, SLOTS = 0, 128, 224, 320, 368, 416, 464, 592
HALO = SLOTS - NORTH
GROUPS = 4
NEG = -1e30


def nt(a, b):
    return lax.dot_general(a, b, (((1,), (1,)), ((), ())), preferred_element_type=F32)


def tn(a, b):
    return lax.dot_general(a, b, (((0,), (0,)), ((), ())), preferred_element_type=F32)


def nn(a, b):
    return lax.dot_general(a, b, (((1,), (0,)), ((), ())), preferred_element_type=F32)


def sixth(t):
    return (t * 43) >> 8


def place(slot, outer_col, inner_col):
    far = 1000
    s = slot - OUTER
    six = jnp.where(s < 48, s, jnp.where(s < 96, s - 48, s - 96))
    outer_row = sixth(six)
    outer_row = jnp.where(s < 48, outer_row, jnp.where(s < 96, outer_row - 8, outer_row + 8))
    t = slot - INNER
    u = jnp.where(t < 48, t, jnp.where(t < 84, t - 48, t - 84))
    inner_row = sixth(u)
    inner_row = jnp.where(
        t < 48, inner_row, jnp.where(t < 84, inner_row - REACH, jnp.where(t < 120, inner_row + 8, far))
    )
    wide = slot >> 4
    wide_row = jnp.where(slot < NORTH, wide, jnp.where(slot < SOUTH, wide - 14, wide - 6))
    row = jnp.where(slot < OUTER, wide_row, jnp.where(slot < INNER, outer_row, inner_row))
    col = jnp.where(
        slot < OUTER,
        slot & 15,
        jnp.where(slot < INNER, outer_col + six - 6 * sixth(six), inner_col + u - 6 * sixth(u)),
    )
    return row, col


def kernel(
    lats, lons, k_in, v_in, q_in, g_in, att_out, dq_out, dk_out, dv_out,
    buf, osend, isend, bias1, bias2, own_stat, send_stat, recv_stat, halo_stat,
    att, dq, dk, dv, dk_own, dv_own,
    in_sem, out_sem, lat_s, lat_r, out_s, out_r, cor_s, cor_r, inn_s, inn_r, st_s, st_r,
):
    lat, lon = lax.axis_index("lat"), lax.axis_index("lon")
    core = lax.rem(lon, 2)
    has_n, has_s = lat > 0, lat < lats - 1
    north, south = jnp.maximum(lat - 1, 0), jnp.minimum(lat + 1, lats - 1)
    outer = jnp.where(core == 0, lax.rem(lon + lons - 1, lons), lax.rem(lon + 1, lons))
    inner = jnp.where(core == 0, lon + 1, lon - 1)
    outer_col = jnp.where(core == 0, -REACH, 16)
    inner_col = jnp.where(core == 0, 16, -REACH)
    outer_first = jnp.where(core == 0, 0, 16 - REACH)
    inner_first = jnp.where(core == 0, 16 - REACH, 0)

    loads = [
        pltpu.make_async_copy(x, buf.at[i, OWN:NORTH, :], in_sem.at[i])
        for i, x in enumerate((k_in, v_in, q_in, g_in))
    ]
    for load in loads:
        load.start()

    barrier = pltpu.get_barrier_semaphore()
    for col in (outer, inner):
        pl.semaphore_signal(barrier, inc=1, device_id={"lon": col}, device_id_type=MESH)
    for col in (lon, outer, inner):
        @pl.when(has_n)
        def _():
            pl.semaphore_signal(
                barrier, inc=1, device_id={"lat": north, "lon": col}, device_id_type=MESH
            )

        @pl.when(has_s)
        def _():
            pl.semaphore_signal(
                barrier, inc=1, device_id={"lat": south, "lon": col}, device_id_type=MESH
            )

    @pl.when(jnp.logical_not(has_n))
    def _():
        buf[:, NORTH:SOUTH, :] = jnp.zeros((4, SOUTH - NORTH, 1024), BF16)
        buf[:, OUTER_N:OUTER_S, :] = jnp.zeros((4, 48, 1024), BF16)

    @pl.when(jnp.logical_not(has_s))
    def _():
        buf[:, SOUTH:OUTER, :] = jnp.zeros((4, OUTER - SOUTH, 1024), BF16)
        buf[:, OUTER_S:INNER, :] = jnp.zeros((4, 48, 1024), BF16)

    recv_stat[...] = jnp.zeros(recv_stat.shape, F32)

    pl.semaphore_wait(barrier, 2 + 3 * jnp.where(has_n, 1, 0) + 3 * jnp.where(has_s, 1, 0))

    for load in loads:
        load.wait()

    width = 1024 // GROUPS

    def lanes(g):
        return pl.ds(pl.multiple_of(g * width, width), width)

    def lat_copy(to_north, ph, g):
        src, dst = (OWN, SOUTH) if to_north else (OWN + 32, NORTH)
        d = 0 if to_north else 1
        return pltpu.make_async_remote_copy(
            buf.at[2 * ph : 2 * ph + 2, src : src + 96, lanes(g)],
            buf.at[2 * ph : 2 * ph + 2, dst : dst + 96, lanes(g)],
            lat_s.at[d, ph, g],
            lat_r.at[d, ph, g],
            device_id={"lat": north if to_north else south},
            device_id_type=MESH,
        )

    def corner_copy(to_north, ph, g):
        dst = OUTER_S if to_north else OUTER_N
        d = 0 if to_north else 1
        return pltpu.make_async_remote_copy(
            buf.at[2 * ph : 2 * ph + 2, OUTER : OUTER + 48, lanes(g)],
            buf.at[2 * ph : 2 * ph + 2, dst : dst + 48, lanes(g)],
            cor_s.at[d, ph, g],
            cor_r.at[d, ph, g],
            device_id={"lat": north if to_north else south},
            device_id_type=MESH,
        )

    def outer_copy(ph):
        return pltpu.make_async_remote_copy(
            osend.at[2 * ph : 2 * ph + 2],
            buf.at[2 * ph : 2 * ph + 2, OUTER : OUTER + 48, :],
            out_s.at[ph],
            out_r.at[ph],
            device_id={"lon": outer},
            device_id_type=MESH,
        )

    def inner_copy(ph, g):
        return pltpu.make_async_remote_copy(
            isend.at[2 * ph : 2 * ph + 2, :, lanes(g)],
            buf.at[2 * ph : 2 * ph + 2, INNER:SLOTS, lanes(g)],
            inn_s.at[ph, g],
            inn_r.at[ph, g],
            device_id={"lon": inner},
            device_id_type=MESH,
        )

    def stat_copy(i):
        lat_to, lon_to, part = (
            (north, lon, 0), (south, lon, 1),
            (lat, outer, 2), (north, outer, 2), (south, outer, 2),
            (lat, inner, 3), (north, inner, 4), (south, inner, 5),
        )[i]
        return pltpu.make_async_remote_copy(
            send_stat.at[part],
            recv_stat.at[i],
            st_s.at[i],
            st_r.at[i],
            device_id={"lat": lat_to, "lon": lon_to},
            device_id_type=MESH,
        )

    def each_group(f):
        def step(g, carry):
            f(g)
            return carry

        lax.fori_loop(0, GROUPS, step, 0)

    def start_both(copy, ph):
        @pl.when(has_n)
        def _():
            each_group(lambda g: copy(True, ph, g).start())

        @pl.when(has_s)
        def _():
            each_group(lambda g: copy(False, ph, g).start())

    start_both(lat_copy, 0)

    slot = lax.broadcasted_iota(jnp.int32, (48, 128), 0)
    patch = lax.broadcasted_iota(jnp.int32, (48, 128), 1)
    row6 = sixth(slot)
    at = row6 * 16 + slot - 6 * row6
    pick_outer = jnp.where(patch == at + outer_first, 1.0, 0.0).astype(BF16)
    pick_inner = jnp.where(patch == at + inner_first, 1.0, 0.0).astype(BF16)
    slot = lax.broadcasted_iota(jnp.int32, (80, 192), 0)
    patch = lax.broadcasted_iota(jnp.int32, (80, 192), 1)
    row6 = sixth(slot)
    at = row6 * 16 + slot - 6 * row6
    pick_rim = jnp.where((patch == at + inner_first) & (slot < 72), 1.0, 0.0).astype(BF16)

    for ph in range(2):
        for i in (2 * ph, 2 * ph + 1):
            osend[i] = nn(pick_outer, buf[i, OWN:NORTH, :]).astype(BF16)
        outer_copy(ph).start()
    for i in range(4):
        isend[i, 0:48, :] = nn(pick_inner, buf[i, OWN:NORTH, :]).astype(BF16)

    first_row = lat * 8

    def bias(shape, key_axis, first_key, first_query):
        row_k, col_k = place(
            lax.broadcasted_iota(jnp.int32, shape, key_axis) + first_key, outer_col, inner_col
        )
        row_q, col_q = place(
            lax.broadcasted_iota(jnp.int32, shape, 1 - key_axis) + first_query, outer_col, inner_col
        )
        ok = (jnp.abs(row_k - row_q) <= REACH) & (jnp.abs(col_k - col_q) <= REACH)
        for row in (row_k, row_q):
            ok = ok & (row + first_row >= 0) & (row + first_row < 8 * lats)
        return jnp.where(ok, 0.0, NEG)

    bias1[...] = bias((SLOTS, 128), 0, 0, 0)
    bias2[...] = bias((128, HALO), 0, 0, NORTH)

    outer_copy(0).wait_recv()
    start_both(corner_copy, 0)
    start_both(lat_copy, 1)
    outer_copy(1).wait_recv()
    start_both(corner_copy, 1)

    def rim(ph, g):
        @pl.when(has_s)
        def _():
            lat_copy(True, ph, g).wait_recv()

        @pl.when(has_n)
        def _():
            lat_copy(False, ph, g).wait_recv()

        for i in (2 * ph, 2 * ph + 1):
            isend[i, 48:128, lanes(g)] = nn(pick_rim, buf[i, NORTH:OUTER, lanes(g)]).astype(BF16)
        inner_copy(ph, g).start()

    def arrive(ph, g):
        @pl.when(has_s)
        def _():
            corner_copy(True, ph, g).wait_recv()

        @pl.when(has_n)
        def _():
            corner_copy(False, ph, g).wait_recv()

        inner_copy(ph, g).wait_recv()

    lane = lax.broadcasted_iota(jnp.int32, (128, 128), 1)
    low = jnp.where(lane < HD, 1.0, 0.0).astype(BF16)
    high = jnp.where(lane < HD, 0.0, 1.0).astype(BF16)
    low_f, high_f = low.astype(F32), high.astype(F32)

    def split(x):
        return jnp.concatenate((x * low, x * high), axis=0)

    def joined(x):
        return jnp.concatenate((x[:HD, :128], x[HD:, 128:]), axis=0).T

    def pair_lanes(p):
        return pl.ds(pl.multiple_of(p * 128, 128), 128)

    def first_pass(p):
        at = pair_lanes(p)
        keys, values = buf[0, :, at], buf[1, :, at]
        queries = split(buf[2, OWN:NORTH, at] * jnp.asarray(0.125, BF16))
        upstream = split(buf[3, OWN:NORTH, at])
        near = bias1[...]
        scores = nt(keys, queries) + jnp.concatenate((near, near), axis=1)
        peak = jnp.max(scores, axis=0, keepdims=True)
        e = jnp.exp(scores - peak)
        total = jnp.sum(e, axis=0, keepdims=True)
        probs = e * (1.0 / total)
        prob_grad = nt(values, upstream)
        delta = jnp.sum(probs * prob_grad, axis=0, keepdims=True)
        score_grad = (probs * (prob_grad - delta)).astype(BF16)
        probs_low = probs.astype(BF16)
        att[:, at] = joined(tn(values, probs_low)).astype(BF16)
        dq[:, at] = (joined(tn(keys, score_grad)) * 0.125).astype(BF16)
        dv_own[:, at] = nn(probs_low[OWN:NORTH], upstream)
        dk_own[:, at] = nn(score_grad[OWN:NORTH], queries)
        log_total = peak + jnp.log(total)
        own_stat[pl.ds(2 * p, 1), :] = log_total[:, :128]
        own_stat[pl.ds(2 * p + 1, 1), :] = log_total[:, 128:]
        own_stat[pl.ds(2 * p + 16, 1), :] = delta[:, :128]
        own_stat[pl.ds(2 * p + 17, 1), :] = delta[:, 128:]

    def second_pass(p):
        at = pair_lanes(p)
        keys = split(buf[0, OWN:NORTH, at] * jnp.asarray(0.125, BF16))
        values = split(buf[1, OWN:NORTH, at])
        queries, upstream = buf[2, NORTH:SLOTS, at], buf[3, NORTH:SLOTS, at]
        scores = nt(keys, queries)
        prob_grad = nt(values, upstream)
        near = bias2[...]
        lows, grads = [], []
        for h in range(2):
            here = slice(128 * h, 128 * h + 128)
            probs = jnp.exp(scores[here] + near - halo_stat[pl.ds(2 * p + h, 1), :])
            lows.append(probs.astype(BF16))
            grads.append((probs * (prob_grad[here] - halo_stat[pl.ds(2 * p + 16 + h, 1), :])).astype(BF16))
        value_part = nn(jnp.concatenate(lows, axis=0), upstream)
        key_part = nn(jnp.concatenate(grads, axis=0), queries)
        value_part = value_part[:128] * low_f + value_part[128:] * high_f
        key_part = key_part[:128] * low_f + key_part[128:] * high_f
        dv[:, at] = (dv_own[:, at] + value_part).astype(BF16)
        dk[:, at] = (dk_own[:, at] + key_part * 0.125).astype(BF16)

    def pairs_of(g, f):
        per = 8 // GROUPS

        def step(i, carry):
            f(g * per + i)
            return carry

        lax.fori_loop(0, per, step, 0)

    rim(0, 0)

    def first_group(g):
        @pl.when(g + 1 < GROUPS)
        def _():
            rim(0, g + 1)

        arrive(0, g)
        pairs_of(g, first_pass)

    each_group(first_group)

    s = own_stat[...]
    hi = s.astype(BF16)
    rest = s - hi.astype(F32)
    mid = rest.astype(BF16)
    parts = jnp.concatenate((hi, mid, (rest - mid.astype(F32)).astype(BF16)), axis=0)

    patch = lax.broadcasted_iota(jnp.int32, (128, 128), 0)
    slot = lax.broadcasted_iota(jnp.int32, (128, 128), 1)

    def spread(shift, first, skip_rows, count):
        t = slot - shift
        r = sixth(jnp.maximum(t, 0))
        want = (r + skip_rows) * 16 + t - 6 * r + first
        pick = jnp.where((t >= 0) & (t < count) & (patch == want), 1.0, 0.0).astype(BF16)
        x = nn(parts, pick)
        return x[0:32] + x[32:64] + x[64:96]

    pick = jnp.where(patch == slot + 32, 1.0, 0.0).astype(BF16)
    x = nn(parts, pick)
    send_stat[0] = s
    send_stat[1] = x[0:32] + x[32:64] + x[64:96]
    send_stat[2] = spread(0, outer_first, 0, 48)
    send_stat[3] = spread(0, inner_first, 0, 48)
    send_stat[4] = spread(84, inner_first, 0, 36)
    send_stat[5] = spread(48, inner_first, 2, 36)

    goes = (has_n, has_s, None, has_n, has_s, None, has_n, has_s)
    comes = (has_s, has_n, None, has_s, has_n, None, has_s, has_n)

    def maybe(cond, f):
        if cond is None:
            f()
        else:
            pl.when(cond)(f)

    for i in range(8):
        maybe(goes[i], lambda i=i: stat_copy(i).start())

    stores = [
        pltpu.make_async_copy(att, att_out, out_sem.at[0]),
        pltpu.make_async_copy(dq, dq_out, out_sem.at[1]),
    ]
    for store in stores:
        store.start()

    rim(1, 0)

    for i in range(8):
        maybe(comes[i], lambda i=i: stat_copy(i).wait_recv())
    from_inner = recv_stat[5] + recv_stat[6] + recv_stat[7]
    halo_stat[...] = jnp.concatenate(
        (
            recv_stat[1][:, :96], recv_stat[0][:, :96], recv_stat[2][:, :48],
            recv_stat[4][:, :48], recv_stat[3][:, :48], from_inner,
        ),
        axis=1,
    )

    def second_group(g):
        @pl.when(g + 1 < GROUPS)
        def _():
            rim(1, g + 1)

        arrive(1, g)
        pairs_of(g, second_pass)

    each_group(second_group)

    stores += [
        pltpu.make_async_copy(dk, dk_out, out_sem.at[2]),
        pltpu.make_async_copy(dv, dv_out, out_sem.at[3]),
    ]
    for store in stores[2:]:
        store.start()

    for ph in range(2):
        for copy in (lat_copy, corner_copy):
            @pl.when(has_n)
            def _():
                each_group(lambda g: copy(True, ph, g).wait_send())

            @pl.when(has_s)
            def _():
                each_group(lambda g: copy(False, ph, g).wait_send())

        outer_copy(ph).wait_send()
        each_group(lambda g: inner_copy(ph, g).wait_send())
    for i in range(8):
        maybe(goes[i], lambda i=i: stat_copy(i).wait_send())
    for store in stores:
        store.wait()


def body(lats, lons, queries, keys, values, cotangent):
    flat = [x.reshape(128, 1024) for x in (keys, values, queries, cotangent)]
    dma = pltpu.SemaphoreType.DMA
    outs = pl.pallas_call(
        functools.partial(kernel, lats, lons),
        out_shape=[jax.ShapeDtypeStruct((128, 1024), BF16)] * 4,
        in_specs=[pl.BlockSpec(memory_space=pl.ANY)] * 4,
        out_specs=[pl.BlockSpec(memory_space=pl.ANY)] * 4,
        scratch_shapes=[
            pltpu.VMEM((4, SLOTS, 1024), BF16),
            pltpu.VMEM((4, 48, 1024), BF16),
            pltpu.VMEM((4, 128, 1024), BF16),
            pltpu.VMEM((SLOTS, 128), F32),
            pltpu.VMEM((128, HALO), F32),
            pltpu.VMEM((32, 128), F32),
            pltpu.VMEM((6, 32, 128), F32),
            pltpu.VMEM((8, 32, 128), F32),
            pltpu.VMEM((32, HALO), F32),
            pltpu.VMEM((128, 1024), BF16),
            pltpu.VMEM((128, 1024), BF16),
            pltpu.VMEM((128, 1024), BF16),
            pltpu.VMEM((128, 1024), BF16),
            pltpu.VMEM((128, 1024), F32),
            pltpu.VMEM((128, 1024), F32),
            dma((4,)),
            dma((4,)),
            dma((2, 2, GROUPS)),
            dma((2, 2, GROUPS)),
            dma((2,)),
            dma((2,)),
            dma((2, 2, GROUPS)),
            dma((2, 2, GROUPS)),
            dma((2, GROUPS)),
            dma((2, GROUPS)),
            dma((8,)),
            dma((8,)),
        ],
        compiler_params=pltpu.CompilerParams(
            collective_id=0, has_side_effects=True, vmem_limit_bytes=48 << 20
        ),
    )(*flat)
    return tuple(x.reshape(8, 16, 1024) for x in outs)


def solution(mesh):
    spec = P("lat", "lon", None)
    return jax.shard_map(
        functools.partial(body, mesh.shape["lat"], mesh.shape["lon"]),
        mesh=mesh,
        in_specs=(spec,) * 4,
        out_specs=(spec,) * 4,
        check_vma=False,
    )
```

time: 169 us -> 77.4 us (0.46)
  the two profiles are of different devices: /device:TPU:64 before, /device:TPU:1 now
where the time goes in v1:
time: 77.4 us; the launch traced here: 77.1 us
  Pallas kernels  69.9 us (90%)
  local copies, waits for them, and re-layouts  6.6 us (9%)
    pallas_call x1, Pallas kernels, body(): pl.pallas_call(functools.partial(kernel, lats, lons), out_shape=[jax.Shap...  69.9 us
    unnamed x12, local copies, waits for them, and re-layouts  6.6 us

profile of v1, /device:TPU:1, one launch (start us, length us, event | category | flops | bytes accessed | tf_op | source)
XLA Modules:
  0.0 77.1 jit_solution(14396996948295063820)
XLA Ops:
  0.6 0.0 copy-start
  0.6 0.9 %copy-done = bf16[8,16,1024]{2,1,0:T(8,128)(2,1)S(1)} copy-done((bf16[8,16,1024]{2,1,0:T(8,128)(2,1)S(1)}, bf16[8,16,1024]{2,1,0:T(8,128)(2,1)}, u32[]{:S(2)}) %copy-start) | copy-done | bytes 262168
  1.6 0.0 copy-start.1
  1.6 0.9 %copy-done.1 = bf16[8,16,1024]{2,1,0:T(8,128)(2,1)S(1)} copy-done((bf16[8,16,1024]{2,1,0:T(8,128)(2,1)S(1)}, bf16[8,16,1024]{2,1,0:T(8,128)(2,1)}, u32[]{:S(2)}) %copy-start.1) | copy-done | bytes 262168
  2.5 0.0 copy-start.2
  2.5 0.9 %copy-done.2 = bf16[8,16,1024]{2,1,0:T(8,128)(2,1)S(1)} copy-done((bf16[8,16,1024]{2,1,0:T(8,128)(2,1)S(1)}, bf16[8,16,1024]{2,1,0:T(8,128)(2,1)}, u32[]{:S(2)}) %copy-start.2) | copy-done | bytes 262168
  3.5 0.0 copy-start.3
  3.5 0.9 %copy-done.3 = bf16[8,16,1024]{2,1,0:T(8,128)(2,1)S(1)} copy-done((bf16[8,16,1024]{2,1,0:T(8,128)(2,1)S(1)}, bf16[8,16,1024]{2,1,0:T(8,128)(2,1)}, u32[]{:S(2)}) %copy-start.3) | copy-done | bytes 262168
  4.4 69.9 %shard_map.75 = (bf16[128,1024]{1,0:T(8,128)(2,1)S(1)}, bf16[128,1024]{1,0:T(8,128)(2,1)S(1)}, bf16[128,1024]{1,0:T(8,128)(2,1)S(1)}, bf16[128,1024]{1,0:T(8,128)(2,1)S(1)}) custom-call(bf16[128,1024]{1,0:T(8,128)(2,1)S(1)} %bitcast.12, bf16[128,1024]{1,0:T(8,128)(2,1)S(1)} %bitcast.13, bf16[128,1024]{1,0:T(8,128)(2,1)S(1)} %bitcast.14, ...), custom_call_target="tpu_custom_call" | custom-call | tf_op jit(solution)/shard_map/pallas_call | solution.py:443
  74.3 0.7 copy.12
  75.0 0.7 copy.13
  75.7 0.7 copy.14
  76.4 0.7 copy.15
Async XLA Ops:
  0.6 1.0 %copy-start = (bf16[8,16,1024]{2,1,0:T(8,128)(2,1)S(1)}, bf16[8,16,1024]{2,1,0:T(8,128)(2,1)}, u32[]{:S(2)}) copy-start(bf16[8,16,1024]{2,1,0:T(8,128)(2,1)} %param.5) | copy-start | bytes 786436
  1.6 0.9 %copy-start.1 = (bf16[8,16,1024]{2,1,0:T(8,128)(2,1)S(1)}, bf16[8,16,1024]{2,1,0:T(8,128)(2,1)}, u32[]{:S(2)}) copy-start(bf16[8,16,1024]{2,1,0:T(8,128)(2,1)} %param.6) | copy-start | bytes 786436
  2.5 0.9 %copy-start.2 = (bf16[8,16,1024]{2,1,0:T(8,128)(2,1)S(1)}, bf16[8,16,1024]{2,1,0:T(8,128)(2,1)}, u32[]{:S(2)}) copy-start(bf16[8,16,1024]{2,1,0:T(8,128)(2,1)} %param.4) | copy-start | bytes 786436
  3.5 0.9 %copy-start.3 = (bf16[8,16,1024]{2,1,0:T(8,128)(2,1)S(1)}, bf16[8,16,1024]{2,1,0:T(8,128)(2,1)}, u32[]{:S(2)}) copy-start(bf16[8,16,1024]{2,1,0:T(8,128)(2,1)} %param.7) | copy-start | bytes 786436

commit v2 on v1

--- a/solution.py
+++ b/solution.py
@@ -16,6 +16,8 @@
 OWN, NORTH, SOUTH, OUTER, OUTER_N, OUTER_S, INNER, SLOTS = 0, 128, 224, 320, 368, 416, 464, 592
 HALO = SLOTS - NORTH
 GROUPS = 4
+CHUNK = 208
+AHEAD = 2
 NEG = -1e30
 
 
@@ -59,17 +61,24 @@
 
 
 def kernel(
-    lats, lons, k_in, v_in, q_in, g_in, att_out, dq_out, dk_out, dv_out,
+    lats, lons, k_in, v_in, q_in, g_in, outs,
     buf, osend, isend, bias1, bias2, own_stat, send_stat, recv_stat, halo_stat,
-    att, dq, dk, dv, dk_own, dv_own,
-    in_sem, out_sem, lat_s, lat_r, out_s, out_r, cor_s, cor_r, inn_s, inn_r, st_s, st_r,
+    att, dq, dk, dv, dk_own, dv_own, work, work2, low_probs, low_grads,
+    ready, in_sem, out_sem, lat_s, lat_r, out_s, out_r, cor_s, cor_r, inn_s, inn_r, st_s, st_r,
 ):
     lat, lon = lax.axis_index("lat"), lax.axis_index("lon")
     core = lax.rem(lon, 2)
     has_n, has_s = lat > 0, lat < lats - 1
+    half = lats // 2
+    far_s, far_n = lat == half - 1, lat == half
+    first, last = lat == 0, lat == lats - 1
+    meets = far_s | far_n | first | last
     north, south = jnp.maximum(lat - 1, 0), jnp.minimum(lat + 1, lats - 1)
     outer = jnp.where(core == 0, lax.rem(lon + lons - 1, lons), lax.rem(lon + 1, lons))
     inner = jnp.where(core == 0, lon + 1, lon - 1)
+    turn = lax.rem(lon, 8)
+    late = turn == 0
+    asks = late | ((core == 1) & (turn < 7))
     outer_col = jnp.where(core == 0, -REACH, 16)
     inner_col = jnp.where(core == 0, 16, -REACH)
     outer_first = jnp.where(core == 0, 0, 16 - REACH)
@@ -82,22 +91,6 @@
     for load in loads:
         load.start()
 
-    barrier = pltpu.get_barrier_semaphore()
-    for col in (outer, inner):
-        pl.semaphore_signal(barrier, inc=1, device_id={"lon": col}, device_id_type=MESH)
-    for col in (lon, outer, inner):
-        @pl.when(has_n)
-        def _():
-            pl.semaphore_signal(
-                barrier, inc=1, device_id={"lat": north, "lon": col}, device_id_type=MESH
-            )
-
-        @pl.when(has_s)
-        def _():
-            pl.semaphore_signal(
-                barrier, inc=1, device_id={"lat": south, "lon": col}, device_id_type=MESH
-            )
-
     @pl.when(jnp.logical_not(has_n))
     def _():
         buf[:, NORTH:SOUTH, :] = jnp.zeros((4, SOUTH - NORTH, 1024), BF16)
@@ -110,7 +103,46 @@
 
     recv_stat[...] = jnp.zeros(recv_stat.shape, F32)
 
-    pl.semaphore_wait(barrier, 2 + 3 * jnp.where(has_n, 1, 0) + 3 * jnp.where(has_s, 1, 0))
+    barrier = pltpu.get_barrier_semaphore()
+    def greet(sem, col, with_row):
+        if with_row:
+            pl.semaphore_signal(sem, inc=1, device_id={"lon": col}, device_id_type=MESH)
+
+        @pl.when(has_n)
+        def _():
+            pl.semaphore_signal(
+                sem, inc=1, device_id={"lat": north, "lon": col}, device_id_type=MESH
+            )
+
+        @pl.when(has_s)
+        def _():
+            pl.semaphore_signal(
+                sem, inc=1, device_id={"lat": south, "lon": col}, device_id_type=MESH
+            )
+
+    greet(barrier, lon, False)
+    greet(barrier, inner, True)
+
+    @pl.when(asks)
+    def _():
+        greet(barrier, outer, True)
+
+    for a in (0, 1):
+        to = jnp.where(far_s | far_n, (0, lats - 1)[a], half - 1 + a)
+
+        @pl.when(meets)
+        def _():
+            pl.semaphore_signal(barrier, inc=1, device_id={"lat": to}, device_id_type=MESH)
+
+    rows = jnp.where(has_n, 1, 0) + jnp.where(has_s, 1, 0)
+    pl.semaphore_wait(
+        barrier,
+        2 * rows + 1 + jnp.where(asks, 0, rows + 1) + 2 * jnp.where(meets, 1, 0),
+    )
+
+    @pl.when(jnp.logical_not(asks))
+    def _():
+        greet(ready, outer, True)
 
     for load in loads:
         load.wait()
@@ -120,29 +152,77 @@
     def lanes(g):
         return pl.ds(pl.multiple_of(g * width, width), width)
 
-    def lat_copy(to_north, ph, g):
-        src, dst = (OWN, SOUTH) if to_north else (OWN + 32, NORTH)
-        d = 0 if to_north else 1
+    def lat_move(sends, recvs, src, dst, ph, g, to_north, lands_north, to):
+        rows = 96 if sends is lat_s else 48
         return pltpu.make_async_remote_copy(
-            buf.at[2 * ph : 2 * ph + 2, src : src + 96, lanes(g)],
-            buf.at[2 * ph : 2 * ph + 2, dst : dst + 96, lanes(g)],
-            lat_s.at[d, ph, g],
-            lat_r.at[d, ph, g],
-            device_id={"lat": north if to_north else south},
+            buf.at[2 * ph : 2 * ph + 2, src : src + rows, lanes(g)],
+            buf.at[2 * ph : 2 * ph + 2, dst : dst + rows, lanes(g)],
+            sends.at[0 if to_north else 1, ph, g],
+            recvs.at[1 if lands_north else 0, ph, g],
+            device_id={"lat": to},
             device_id_type=MESH,
         )
 
-    def corner_copy(to_north, ph, g):
-        dst = OUTER_S if to_north else OUTER_N
-        d = 0 if to_north else 1
-        return pltpu.make_async_remote_copy(
-            buf.at[2 * ph : 2 * ph + 2, OUTER : OUTER + 48, lanes(g)],
-            buf.at[2 * ph : 2 * ph + 2, dst : dst + 48, lanes(g)],
-            cor_s.at[d, ph, g],
-            cor_r.at[d, ph, g],
-            device_id={"lat": north if to_north else south},
-            device_id_type=MESH,
-        )
+    def lat_copy(to_north, ph, g, way="direct"):
+        own = OWN if to_north else OWN + 32
+        above, below = NORTH, SOUTH
+        return by_way(lat_s, lat_r, own, above, below, to_north, ph, g, way)
+
+    def corner_copy(to_north, ph, g, way="direct"):
+        return by_way(cor_s, cor_r, OUTER, OUTER_N, OUTER_S, to_north, ph, g, way)
+
+    def by_way(sends, recvs, own, above, below, to_north, ph, g, way):
+        if way == "direct":
+            to = north if to_north else south
+            return lat_move(
+                sends, recvs, own, below if to_north else above, ph, g, to_north, not to_north, to
+            )
+        if way == "detour":
+            to = 0 if to_north else lats - 1
+            return lat_move(
+                sends, recvs, own, above if to_north else below, ph, g, to_north, to_north, to
+            )
+        to = half - 1 if to_north else half
+        src, dst = (above, below) if to_north else (below, above)
+        return lat_move(sends, recvs, src, dst, ph, g, to_north, not to_north, to)
+
+    def send(copy, to_north, ph, g):
+        has = has_n if to_north else has_s
+        detour = (far_n if to_north else far_s) & (g % 2 == 1)
+
+        @pl.when(has & jnp.logical_not(detour))
+        def _():
+            copy(to_north, ph, g).start()
+
+        @pl.when(detour)
+        def _():
+            copy(to_north, ph, g, "detour").start()
+
+    def wait_sent(copy, to_north, ph, g):
+        @pl.when((has_n | (g % 2 == 1)) if to_north else (has_s | (g % 2 == 1)))
+        def _():
+            copy(to_north, ph, g).wait_send()
+
+    def receive(copy, ph, g):
+        @pl.when(has_s)
+        def _():
+            copy(True, ph, g).wait_recv()
+
+        @pl.when(has_n)
+        def _():
+            copy(False, ph, g).wait_recv()
+
+    def pass_on(copy, ph, groups=range(1, GROUPS, 2)):
+        for g in groups:
+            @pl.when(first)
+            def _():
+                copy(False, ph, g).wait_recv()
+                copy(True, ph, g, "onward").start()
+
+            @pl.when(last)
+            def _():
+                copy(True, ph, g).wait_recv()
+                copy(False, ph, g, "onward").start()
 
     def outer_copy(ph):
         return pltpu.make_async_remote_copy(
@@ -179,23 +259,25 @@
             device_id_type=MESH,
         )
 
-    def each_group(f):
+    def each_group(f, start=0, stop=GROUPS):
         def step(g, carry):
             f(g)
             return carry
 
-        lax.fori_loop(0, GROUPS, step, 0)
-
-    def start_both(copy, ph):
-        @pl.when(has_n)
-        def _():
-            each_group(lambda g: copy(True, ph, g).start())
-
-        @pl.when(has_s)
-        def _():
-            each_group(lambda g: copy(False, ph, g).start())
+        lax.fori_loop(start, stop, step, 0)
+
+    def start_both(copy, ph, start=0, stop=GROUPS):
+        def one(g):
+            send(copy, True, ph, g)
+            send(copy, False, ph, g)
+
+        each_group(one, start, stop)
 
     start_both(lat_copy, 0)
+
+    @pl.when(late)
+    def _():
+        start_both(lat_copy, 1)
 
     slot = lax.broadcasted_iota(jnp.int32, (48, 128), 0)
     patch = lax.broadcasted_iota(jnp.int32, (48, 128), 1)
@@ -209,12 +291,27 @@
     at = row6 * 16 + slot - 6 * row6
     pick_rim = jnp.where((patch == at + inner_first) & (slot < 72), 1.0, 0.0).astype(BF16)
 
-    for ph in range(2):
+    def rim(ph, g):
+        receive(lat_copy, ph, g)
         for i in (2 * ph, 2 * ph + 1):
-            osend[i] = nn(pick_outer, buf[i, OWN:NORTH, :]).astype(BF16)
-        outer_copy(ph).start()
+            isend[i, 48:128, lanes(g)] = nn(pick_rim, buf[i, NORTH:OUTER, lanes(g)]).astype(BF16)
+        inner_copy(ph, g).start()
+
     for i in range(4):
+        osend[i] = nn(pick_outer, buf[i, OWN:NORTH, :]).astype(BF16)
         isend[i, 0:48, :] = nn(pick_inner, buf[i, OWN:NORTH, :]).astype(BF16)
+
+    @pl.when(late)
+    def _():
+        pass_on(lat_copy, 0)
+        each_group(lambda g: rim(0, g))
+
+    @pl.when(asks)
+    def _():
+        pl.semaphore_wait(ready, rows + 1)
+
+    outer_copy(0).start()
+    outer_copy(1).start()
 
     first_row = lat * 8
 
@@ -235,32 +332,18 @@
 
     outer_copy(0).wait_recv()
     start_both(corner_copy, 0)
-    start_both(lat_copy, 1)
-    outer_copy(1).wait_recv()
-    start_both(corner_copy, 1)
-
-    def rim(ph, g):
-        @pl.when(has_s)
-        def _():
-            lat_copy(True, ph, g).wait_recv()
-
-        @pl.when(has_n)
-        def _():
-            lat_copy(False, ph, g).wait_recv()
-
-        for i in (2 * ph, 2 * ph + 1):
-            isend[i, 48:128, lanes(g)] = nn(pick_rim, buf[i, NORTH:OUTER, lanes(g)]).astype(BF16)
-        inner_copy(ph, g).start()
+
+    @pl.when(jnp.logical_not(late))
+    def _():
+        start_both(lat_copy, 1, 0, AHEAD)
+        pass_on(lat_copy, 0)
+        each_group(lambda g: rim(0, g))
+
+    pass_on(corner_copy, 0)
+
 
     def arrive(ph, g):
-        @pl.when(has_s)
-        def _():
-            corner_copy(True, ph, g).wait_recv()
-
-        @pl.when(has_n)
-        def _():
-            corner_copy(False, ph, g).wait_recv()
-
+        receive(corner_copy, ph, g)
         inner_copy(ph, g).wait_recv()
 
     lane = lax.broadcasted_iota(jnp.int32, (128, 128), 1)
@@ -282,16 +365,31 @@
         keys, values = buf[0, :, at], buf[1, :, at]
         queries = split(buf[2, OWN:NORTH, at] * jnp.asarray(0.125, BF16))
         upstream = split(buf[3, OWN:NORTH, at])
-        near = bias1[...]
-        scores = nt(keys, queries) + jnp.concatenate((near, near), axis=1)
-        peak = jnp.max(scores, axis=0, keepdims=True)
-        e = jnp.exp(scores - peak)
-        total = jnp.sum(e, axis=0, keepdims=True)
-        probs = e * (1.0 / total)
-        prob_grad = nt(values, upstream)
-        delta = jnp.sum(probs * prob_grad, axis=0, keepdims=True)
-        score_grad = (probs * (prob_grad - delta)).astype(BF16)
-        probs_low = probs.astype(BF16)
+        cuts = [(r, min(r + CHUNK, SLOTS)) for r in range(0, SLOTS, CHUNK)]
+        peak = jnp.full((8, 256), NEG, F32)
+        for lo, hi in cuts:
+            near = bias1[lo:hi]
+            part = nt(keys[lo:hi], queries) + jnp.concatenate((near, near), axis=1)
+            work[lo:hi] = part
+            peak = jnp.maximum(peak, jnp.max(part.reshape(-1, 8, 256), axis=0))
+        peak = jnp.max(peak, axis=0, keepdims=True)
+        total = jnp.zeros((8, 256), F32)
+        delta = jnp.zeros((8, 256), F32)
+        for lo, hi in cuts:
+            e = jnp.exp(work[lo:hi] - peak)
+            part = nt(values[lo:hi], upstream)
+            work[lo:hi] = e
+            work2[lo:hi] = part
+            total = total + jnp.sum(e.reshape(-1, 8, 256), axis=0)
+            delta = delta + jnp.sum((e * part).reshape(-1, 8, 256), axis=0)
+        total = jnp.sum(total, axis=0, keepdims=True)
+        scale = 1.0 / total
+        delta = jnp.sum(delta, axis=0, keepdims=True) * scale
+        for lo, hi in cuts:
+            probs = work[lo:hi] * scale
+            low_probs[lo:hi] = probs.astype(BF16)
+            low_grads[lo:hi] = (probs * (work2[lo:hi] - delta)).astype(BF16)
+        probs_low, score_grad = low_probs[...], low_grads[...]
         att[:, at] = joined(tn(values, probs_low)).astype(BF16)
         dq[:, at] = (joined(tn(keys, score_grad)) * 0.125).astype(BF16)
         dv_own[:, at] = nn(probs_low[OWN:NORTH], upstream)
@@ -325,22 +423,24 @@
 
     def pairs_of(g, f):
         per = 8 // GROUPS
-
-        def step(i, carry):
+        for i in range(per):
             f(g * per + i)
-            return carry
-
-        lax.fori_loop(0, per, step, 0)
-
-    rim(0, 0)
+
+    def outer_rest():
+        outer_copy(1).wait_recv()
+        start_both(corner_copy, 1)
 
     def first_group(g):
-        @pl.when(g + 1 < GROUPS)
-        def _():
-            rim(0, g + 1)
+        @pl.when(late & (g == 2))
+        def _():
+            outer_rest()
 
         arrive(0, g)
         pairs_of(g, first_pass)
+
+        @pl.when(g == 1)
+        def _():
+            pass_on(lat_copy, 1, (1,))
 
     each_group(first_group)
 
@@ -383,13 +483,20 @@
         maybe(goes[i], lambda i=i: stat_copy(i).start())
 
     stores = [
-        pltpu.make_async_copy(att, att_out, out_sem.at[0]),
-        pltpu.make_async_copy(dq, dq_out, out_sem.at[1]),
+        pltpu.make_async_copy(att, outs.at[0], out_sem.at[0]),
+        pltpu.make_async_copy(dq, outs.at[1], out_sem.at[1]),
     ]
     for store in stores:
         store.start()
 
-    rim(1, 0)
+    @pl.when(jnp.logical_not(late))
+    def _():
+        start_both(lat_copy, 1, AHEAD, GROUPS)
+        outer_rest()
+
+    pass_on(lat_copy, 1, (3,))
+    each_group(lambda g: rim(1, g))
+    pass_on(corner_copy, 1)
 
     for i in range(8):
         maybe(comes[i], lambda i=i: stat_copy(i).wait_recv())
@@ -403,31 +510,25 @@
     )
 
     def second_group(g):
-        @pl.when(g + 1 < GROUPS)
-        def _():
-            rim(1, g + 1)
-
         arrive(1, g)
         pairs_of(g, second_pass)
 
     each_group(second_group)
 
     stores += [
-        pltpu.make_async_copy(dk, dk_out, out_sem.at[2]),
-        pltpu.make_async_copy(dv, dv_out, out_sem.at[3]),
+        pltpu.make_async_copy(dk, outs.at[2], out_sem.at[2]),
+        pltpu.make_async_copy(dv, outs.at[3], out_sem.at[3]),
     ]
     for store in stores[2:]:
         store.start()
 
     for ph in range(2):
         for copy in (lat_copy, corner_copy):
-            @pl.when(has_n)
-            def _():
-                each_group(lambda g: copy(True, ph, g).wait_send())
-
-            @pl.when(has_s)
-            def _():
-                each_group(lambda g: copy(False, ph, g).wait_send())
+            def sent(g):
+                wait_sent(copy, True, ph, g)
+                wait_sent(copy, False, ph, g)
+
+            each_group(sent)
 
         outer_copy(ph).wait_send()
         each_group(lambda g: inner_copy(ph, g).wait_send())
@@ -438,13 +539,16 @@
 
 
 def body(lats, lons, queries, keys, values, cotangent):
-    flat = [x.reshape(128, 1024) for x in (keys, values, queries, cotangent)]
+    flat = [
+        pltpu.with_memory_space_constraint(x.reshape(128, 1024), pltpu.HBM)
+        for x in (keys, values, queries, cotangent)
+    ]
     dma = pltpu.SemaphoreType.DMA
     outs = pl.pallas_call(
         functools.partial(kernel, lats, lons),
-        out_shape=[jax.ShapeDtypeStruct((128, 1024), BF16)] * 4,
-        in_specs=[pl.BlockSpec(memory_space=pl.ANY)] * 4,
-        out_specs=[pl.BlockSpec(memory_space=pl.ANY)] * 4,
+        out_shape=jax.ShapeDtypeStruct((4, 128, 1024), BF16),
+        in_specs=[pl.BlockSpec(memory_space=pltpu.HBM)] * 4,
+        out_specs=pl.BlockSpec(memory_space=pl.ANY),
         scratch_shapes=[
             pltpu.VMEM((4, SLOTS, 1024), BF16),
             pltpu.VMEM((4, 48, 1024), BF16),
@@ -461,6 +565,11 @@
             pltpu.VMEM((128, 1024), BF16),
             pltpu.VMEM((128, 1024), F32),
             pltpu.VMEM((128, 1024), F32),
+            pltpu.VMEM((SLOTS, 256), F32),
+            pltpu.VMEM((SLOTS, 256), F32),
+            pltpu.VMEM((SLOTS, 256), BF16),
+            pltpu.VMEM((SLOTS, 256), BF16),
+            pltpu.SemaphoreType.REGULAR,
             dma((4,)),
             dma((4,)),
             dma((2, 2, GROUPS)),
@@ -478,7 +587,7 @@
             collective_id=0, has_side_effects=True, vmem_limit_bytes=48 << 20
         ),
     )(*flat)
-    return tuple(x.reshape(8, 16, 1024) for x in outs)
+    return tuple(outs[i].reshape(8, 16, 1024) for i in range(4))
 
 
 def solution(mesh):

time: 77.4 us -> 51.4 us (0.66)
  the two profiles are of different devices: /device:TPU:1 before, /device:TPU:64 now
where the time goes in v2:
time: 51.4 us; the launch traced here: 51.2 us
  Pallas kernels  49.6 us (96%)
  local copies, waits for them, and re-layouts  0.98 us (2%)
  between operations  0.64 us (1%)
    pallas_call x1, Pallas kernels, body(): pl.pallas_call(functools.partial(kernel, lats, lons), out_shape=jax.Shape...  49.6 us

profile of v2, /device:TPU:64, one launch (start us, length us, event | category | flops | bytes accessed | tf_op | source)
XLA Modules:
  0.0 51.2 jit_solution(18412829243842985346)
XLA Ops:
  0.6 49.6 %shard_map.75 = bf16[4,128,1024]{2,1,0:T(8,128)(2,1)S(1)} custom-call(bf16[128,1024]{1,0:T(8,128)(2,1)} %bitcast.8, bf16[128,1024]{1,0:T(8,128)(2,1)} %bitcast.9, bf16[128,1024]{1,0:T(8,128)(2,1)} %bitcast.10, bf16[128,1024]{1,0:T(8,128)(2,1)} %bitcast.11), custom_call_target="tpu_custom_call" | custom-call | tf_op jit(solution)/shard_map/pallas_call | solution.py:547
  50.2 1.0 %fusion = (bf16[1,128,1024]{2,1,0:T(8,128)(2,1)}, bf16[1,128,1024]{2,1,0:T(8,128)(2,1)}, bf16[1,128,1024]{2,1,0:T(8,128)(2,1)}, bf16[1,128,1024]{2,1,0:T(8,128)(2,1)}) fusion(bf16[4,128,1024]{2,1,0:T(8,128)(2,1)S(1)} %shard_map.75), kind=kLoop, calls=%fused_computation | loop fusion | bytes 2097152 | tf_op jit(solution)/shard_map/slice | solution.py:590

commit v3 on v2

--- a/solution.py
+++ b/solution.py
@@ -16,6 +16,7 @@
 OWN, NORTH, SOUTH, OUTER, OUTER_N, OUTER_S, INNER, SLOTS = 0, 128, 224, 320, 368, 416, 464, 592
 HALO = SLOTS - NORTH
 GROUPS = 4
+PER = 2
 CHUNK = 208
 AHEAD = 2
 NEG = -1e30
@@ -64,7 +65,7 @@
     lats, lons, k_in, v_in, q_in, g_in, outs,
     buf, osend, isend, bias1, bias2, own_stat, send_stat, recv_stat, halo_stat,
     att, dq, dk, dv, dk_own, dv_own, work, work2, low_probs, low_grads,
-    ready, in_sem, out_sem, lat_s, lat_r, out_s, out_r, cor_s, cor_r, inn_s, inn_r, st_s, st_r,
+    picks, ready, in_sem, out_sem, fin_sem, lat_s, lat_r, out_s, out_r, cor_s, cor_r, inn_s, inn_r, st_s, st_r,
 ):
     lat, lon = lax.axis_index("lat"), lax.axis_index("lon")
     core = lax.rem(lon, 2)
@@ -244,17 +245,17 @@
             device_id_type=MESH,
         )
 
-    def stat_copy(i):
+    def stat_copy(i, g):
         lat_to, lon_to, part = (
             (north, lon, 0), (south, lon, 1),
             (lat, outer, 2), (north, outer, 2), (south, outer, 2),
             (lat, inner, 3), (north, inner, 4), (south, inner, 5),
         )[i]
         return pltpu.make_async_remote_copy(
-            send_stat.at[part],
-            recv_stat.at[i],
-            st_s.at[i],
-            st_r.at[i],
+            send_stat.at[g, part],
+            recv_stat.at[g, i],
+            st_s.at[i, g],
+            st_r.at[i, g],
             device_id={"lat": lat_to, "lon": lon_to},
             device_id_type=MESH,
         )
@@ -311,7 +312,11 @@
         pl.semaphore_wait(ready, rows + 1)
 
     outer_copy(0).start()
-    outer_copy(1).start()
+    holds = turn != 7
+
+    @pl.when(jnp.logical_not(holds))
+    def _():
+        outer_copy(1).start()
 
     first_row = lat * 8
 
@@ -330,6 +335,55 @@
     bias1[...] = bias((SLOTS, 128), 0, 0, 0)
     bias2[...] = bias((128, HALO), 0, 0, NORTH)
 
+    patch = lax.broadcasted_iota(jnp.int32, (128, 128), 0)
+    slot = lax.broadcasted_iota(jnp.int32, (128, 128), 1)
+
+    def spread(shift, edge, skip_rows, count):
+        t = slot - shift
+        r = sixth(jnp.maximum(t, 0))
+        want = (r + skip_rows) * 16 + t - 6 * r + edge
+        return jnp.where((t >= 0) & (t < count) & (patch == want), 1.0, 0.0).astype(BF16)
+
+    picks[0] = jnp.where(patch == slot + 32, 1.0, 0.0).astype(BF16)
+    picks[1] = spread(0, outer_first, 0, 48)
+    picks[2] = spread(0, inner_first, 0, 48)
+    picks[3] = spread(84, inner_first, 0, 36)
+    picks[4] = spread(48, inner_first, 2, 36)
+
+    goes = (has_n, has_s, None, has_n, has_s, None, has_n, has_s)
+    comes = (has_s, has_n, None, has_s, has_n, None, has_s, has_n)
+
+    def maybe(cond, f):
+        if cond is None:
+            f()
+        else:
+            pl.when(cond)(f)
+
+    def tell(g):
+        s = own_stat[g]
+        hi = s.astype(BF16)
+        rest = s - hi.astype(F32)
+        mid = rest.astype(BF16).astype(F32)
+        parts = jnp.concatenate((hi.astype(F32), mid, rest - mid), axis=0).astype(BF16)
+        send_stat[g, 0] = s
+        for i in range(5):
+            x = nn(parts, picks[i])
+            send_stat[g, i + 1] = x[0:8] + x[8:16] + x[16:24]
+        for i in range(8):
+            maybe(goes[i], lambda i=i: stat_copy(i, g).start())
+
+    def hear(g):
+        for i in range(8):
+            maybe(comes[i], lambda i=i: stat_copy(i, g).wait_recv())
+        got = recv_stat[g]
+        halo_stat[g] = jnp.concatenate(
+            (
+                got[1][:, :96], got[0][:, :96], got[2][:, :48], got[4][:, :48], got[3][:, :48],
+                got[5] + got[6] + got[7],
+            ),
+            axis=1,
+        )
+
     outer_copy(0).wait_recv()
     start_both(corner_copy, 0)
 
@@ -338,6 +392,10 @@
         start_both(lat_copy, 1, 0, AHEAD)
         pass_on(lat_copy, 0)
         each_group(lambda g: rim(0, g))
+
+    @pl.when(holds)
+    def _():
+        outer_copy(1).start()
 
     pass_on(corner_copy, 0)
 
@@ -360,8 +418,8 @@
     def pair_lanes(p):
         return pl.ds(pl.multiple_of(p * 128, 128), 128)
 
-    def first_pass(p):
-        at = pair_lanes(p)
+    def first_pass(g, i):
+        at = pair_lanes(g * PER + i)
         keys, values = buf[0, :, at], buf[1, :, at]
         queries = split(buf[2, OWN:NORTH, at] * jnp.asarray(0.125, BF16))
         upstream = split(buf[3, OWN:NORTH, at])
@@ -395,13 +453,13 @@
         dv_own[:, at] = nn(probs_low[OWN:NORTH], upstream)
         dk_own[:, at] = nn(score_grad[OWN:NORTH], queries)
         log_total = peak + jnp.log(total)
-        own_stat[pl.ds(2 * p, 1), :] = log_total[:, :128]
-        own_stat[pl.ds(2 * p + 1, 1), :] = log_total[:, 128:]
-        own_stat[pl.ds(2 * p + 16, 1), :] = delta[:, :128]
-        own_stat[pl.ds(2 * p + 17, 1), :] = delta[:, 128:]
-
-    def second_pass(p):
-        at = pair_lanes(p)
+        for h in range(2):
+            here = slice(128 * h, 128 * h + 128)
+            own_stat[g, 2 * i + h : 2 * i + h + 1, :] = log_total[:, here]
+            own_stat[g, 4 + 2 * i + h : 5 + 2 * i + h, :] = delta[:, here]
+
+    def second_pass(g, i):
+        at = pair_lanes(g * PER + i)
         keys = split(buf[0, OWN:NORTH, at] * jnp.asarray(0.125, BF16))
         values = split(buf[1, OWN:NORTH, at])
         queries, upstream = buf[2, NORTH:SLOTS, at], buf[3, NORTH:SLOTS, at]
@@ -411,9 +469,10 @@
         lows, grads = [], []
         for h in range(2):
             here = slice(128 * h, 128 * h + 128)
-            probs = jnp.exp(scores[here] + near - halo_stat[pl.ds(2 * p + h, 1), :])
+            probs = jnp.exp(scores[here] + near - halo_stat[g, 2 * i + h : 2 * i + h + 1, :])
             lows.append(probs.astype(BF16))
-            grads.append((probs * (prob_grad[here] - halo_stat[pl.ds(2 * p + 16 + h, 1), :])).astype(BF16))
+            change = prob_grad[here] - halo_stat[g, 4 + 2 * i + h : 5 + 2 * i + h, :]
+            grads.append((probs * change).astype(BF16))
         value_part = nn(jnp.concatenate(lows, axis=0), upstream)
         key_part = nn(jnp.concatenate(grads, axis=0), queries)
         value_part = value_part[:128] * low_f + value_part[128:] * high_f
@@ -422,9 +481,8 @@
         dk[:, at] = (dk_own[:, at] + key_part * 0.125).astype(BF16)
 
     def pairs_of(g, f):
-        per = 8 // GROUPS
-        for i in range(per):
-            f(g * per + i)
+        for i in range(PER):
+            f(g, i)
 
     def outer_rest():
         outer_copy(1).wait_recv()
@@ -437,50 +495,18 @@
 
         arrive(0, g)
         pairs_of(g, first_pass)
+        tell(g)
+
+        @pl.when(jnp.logical_not(late) & (g >= AHEAD - 1) & (g < GROUPS - 1))
+        def _():
+            send(lat_copy, True, 1, g + 1)
+            send(lat_copy, False, 1, g + 1)
 
         @pl.when(g == 1)
         def _():
             pass_on(lat_copy, 1, (1,))
 
     each_group(first_group)
-
-    s = own_stat[...]
-    hi = s.astype(BF16)
-    rest = s - hi.astype(F32)
-    mid = rest.astype(BF16)
-    parts = jnp.concatenate((hi, mid, (rest - mid.astype(F32)).astype(BF16)), axis=0)
-
-    patch = lax.broadcasted_iota(jnp.int32, (128, 128), 0)
-    slot = lax.broadcasted_iota(jnp.int32, (128, 128), 1)
-
-    def spread(shift, first, skip_rows, count):
-        t = slot - shift
-        r = sixth(jnp.maximum(t, 0))
-        want = (r + skip_rows) * 16 + t - 6 * r + first
-        pick = jnp.where((t >= 0) & (t < count) & (patch == want), 1.0, 0.0).astype(BF16)
-        x = nn(parts, pick)
-        return x[0:32] + x[32:64] + x[64:96]
-
-    pick = jnp.where(patch == slot + 32, 1.0, 0.0).astype(BF16)
-    x = nn(parts, pick)
-    send_stat[0] = s
-    send_stat[1] = x[0:32] + x[32:64] + x[64:96]
-    send_stat[2] = spread(0, outer_first, 0, 48)
-    send_stat[3] = spread(0, inner_first, 0, 48)
-    send_stat[4] = spread(84, inner_first, 0, 36)
-    send_stat[5] = spread(48, inner_first, 2, 36)
-
-    goes = (has_n, has_s, None, has_n, has_s, None, has_n, has_s)
-    comes = (has_s, has_n, None, has_s, has_n, None, has_s, has_n)
-
-    def maybe(cond, f):
-        if cond is None:
-            f()
-        else:
-            pl.when(cond)(f)
-
-    for i in range(8):
-        maybe(goes[i], lambda i=i: stat_copy(i).start())
 
     stores = [
         pltpu.make_async_copy(att, outs.at[0], out_sem.at[0]),
@@ -491,36 +517,28 @@
 
     @pl.when(jnp.logical_not(late))
     def _():
-        start_both(lat_copy, 1, AHEAD, GROUPS)
         outer_rest()
 
     pass_on(lat_copy, 1, (3,))
     each_group(lambda g: rim(1, g))
     pass_on(corner_copy, 1)
 
-    for i in range(8):
-        maybe(comes[i], lambda i=i: stat_copy(i).wait_recv())
-    from_inner = recv_stat[5] + recv_stat[6] + recv_stat[7]
-    halo_stat[...] = jnp.concatenate(
-        (
-            recv_stat[1][:, :96], recv_stat[0][:, :96], recv_stat[2][:, :48],
-            recv_stat[4][:, :48], recv_stat[3][:, :48], from_inner,
-        ),
-        axis=1,
-    )
+    def finals(g):
+        return [
+            pltpu.make_async_copy(
+                x.at[:, lanes(g)], outs.at[2 + i, :, lanes(g)], fin_sem.at[i, g]
+            )
+            for i, x in enumerate((dk, dv))
+        ]
 
     def second_group(g):
+        hear(g)
         arrive(1, g)
         pairs_of(g, second_pass)
+        for copy in finals(g):
+            copy.start()
 
     each_group(second_group)
-
-    stores += [
-        pltpu.make_async_copy(dk, outs.at[2], out_sem.at[2]),
-        pltpu.make_async_copy(dv, outs.at[3], out_sem.at[3]),
-    ]
-    for store in stores[2:]:
-        store.start()
 
     for ph in range(2):
         for copy in (lat_copy, corner_copy):
@@ -533,9 +551,15 @@
         outer_copy(ph).wait_send()
         each_group(lambda g: inner_copy(ph, g).wait_send())
     for i in range(8):
-        maybe(goes[i], lambda i=i: stat_copy(i).wait_send())
+        maybe(goes[i], lambda i=i: each_group(lambda g: stat_copy(i, g).wait_send()))
     for store in stores:
         store.wait()
+
+    def ended(g):
+        for copy in finals(g):
+            copy.wait()
+
+    each_group(ended)
 
 
 def body(lats, lons, queries, keys, values, cotangent):
@@ -555,10 +579,10 @@
             pltpu.VMEM((4, 128, 1024), BF16),
             pltpu.VMEM((SLOTS, 128), F32),
             pltpu.VMEM((128, HALO), F32),
-            pltpu.VMEM((32, 128), F32),
-            pltpu.VMEM((6, 32, 128), F32),
-            pltpu.VMEM((8, 32, 128), F32),
-            pltpu.VMEM((32, HALO), F32),
+            pltpu.VMEM((GROUPS, 8, 128), F32),
+            pltpu.VMEM((GROUPS, 6, 8, 128), F32),
+            pltpu.VMEM((GROUPS, 8, 8, 128), F32),
+            pltpu.VMEM((GROUPS, 8, HALO), F32),
             pltpu.VMEM((128, 1024), BF16),
             pltpu.VMEM((128, 1024), BF16),
             pltpu.VMEM((128, 1024), BF16),
@@ -569,9 +593,11 @@
             pltpu.VMEM((SLOTS, 256), F32),
             pltpu.VMEM((SLOTS, 256), BF16),
             pltpu.VMEM((SLOTS, 256), BF16),
+            pltpu.VMEM((5, 128, 128), BF16),
             pltpu.SemaphoreType.REGULAR,
             dma((4,)),
-            dma((4,)),
+            dma((2,)),
+            dma((2, GROUPS)),
             dma((2, 2, GROUPS)),
             dma((2, 2, GROUPS)),
             dma((2,)),
@@ -580,8 +606,8 @@
             dma((2, 2, GROUPS)),
             dma((2, GROUPS)),
             dma((2, GROUPS)),
-            dma((8,)),
-            dma((8,)),
+            dma((8, GROUPS)),
+            dma((8, GROUPS)),
         ],
         compiler_params=pltpu.CompilerParams(
             collective_id=0, has_side_effects=True, vmem_limit_bytes=48 << 20

time: 51.4 us -> 47.4 us (0.922)
  the two profiles are of different devices: /device:TPU:64 before, /device:TPU:8 now
where the time goes in v3:
time: 47.4 us; the launch traced here: 47.2 us
  Pallas kernels  45.6 us (96%)
  local copies, waits for them, and re-layouts  0.98 us (2%)
  between operations  0.64 us (1%)
    pallas_call x1, Pallas kernels, body(): pl.pallas_call(functools.partial(kernel, lats, lons), out_shape=jax.Shape...  45.6 us
    slice x1, local copies, waits for them, and re-layouts, body(): return tuple((outs[i].reshape(8, 16, 1024) for i in range(4)))  0.98 us

profile of v3, /device:TPU:8, one launch (start us, length us, event | category | flops | bytes accessed | tf_op | source)
XLA Modules:
  0.0 47.2 jit_solution(11649293338275970867)
XLA Ops:
  0.6 45.6 %shard_map.75 = bf16[4,128,1024]{2,1,0:T(8,128)(2,1)S(1)} custom-call(bf16[128,1024]{1,0:T(8,128)(2,1)} %bitcast.8, bf16[128,1024]{1,0:T(8,128)(2,1)} %bitcast.9, bf16[128,1024]{1,0:T(8,128)(2,1)} %bitcast.10, bf16[128,1024]{1,0:T(8,128)(2,1)} %bitcast.11), custom_call_target="tpu_custom_call" | custom-call | tf_op jit(solution)/shard_map/pallas_call | solution.py:571
  46.2 1.0 %fusion = (bf16[1,128,1024]{2,1,0:T(8,128)(2,1)}, bf16[1,128,1024]{2,1,0:T(8,128)(2,1)}, bf16[1,128,1024]{2,1,0:T(8,128)(2,1)}, bf16[1,128,1024]{2,1,0:T(8,128)(2,1)}) fusion(bf16[4,128,1024]{2,1,0:T(8,128)(2,1)S(1)} %shard_map.75), kind=kLoop, calls=%fused_computation | loop fusion | bytes 2097152 | tf_op jit(solution)/shard_map/slice | solution.py:616

commit v4 on v3

--- a/solution.py
+++ b/solution.py
@@ -17,6 +17,7 @@
 HALO = SLOTS - NORTH
 GROUPS = 4
 PER = 2
+TOLD = 2
 CHUNK = 208
 AHEAD = 2
 NEG = -1e30
@@ -360,7 +361,7 @@
             pl.when(cond)(f)
 
     def tell(g):
-        s = own_stat[g]
+        s = own_stat[g].reshape(16, 128)
         hi = s.astype(BF16)
         rest = s - hi.astype(F32)
         mid = rest.astype(BF16).astype(F32)
@@ -368,7 +369,7 @@
         send_stat[g, 0] = s
         for i in range(5):
             x = nn(parts, picks[i])
-            send_stat[g, i + 1] = x[0:8] + x[8:16] + x[16:24]
+            send_stat[g, i + 1] = x[0:16] + x[16:32] + x[32:48]
         for i in range(8):
             maybe(goes[i], lambda i=i: stat_copy(i, g).start())
 
@@ -376,13 +377,17 @@
         for i in range(8):
             maybe(comes[i], lambda i=i: stat_copy(i, g).wait_recv())
         got = recv_stat[g]
-        halo_stat[g] = jnp.concatenate(
+        halo_stat[...] = jnp.concatenate(
             (
                 got[1][:, :96], got[0][:, :96], got[2][:, :48], got[4][:, :48], got[3][:, :48],
                 got[5] + got[6] + got[7],
             ),
             axis=1,
-        )
+        ).reshape(2, 8, HALO)
+
+    @pl.when(jnp.logical_not(late))
+    def _():
+        pass_on(lat_copy, 0, (1,))
 
     outer_copy(0).wait_recv()
     start_both(corner_copy, 0)
@@ -390,7 +395,7 @@
     @pl.when(jnp.logical_not(late))
     def _():
         start_both(lat_copy, 1, 0, AHEAD)
-        pass_on(lat_copy, 0)
+        pass_on(lat_copy, 0, (3,))
         each_group(lambda g: rim(0, g))
 
     @pl.when(holds)
@@ -455,8 +460,8 @@
         log_total = peak + jnp.log(total)
         for h in range(2):
             here = slice(128 * h, 128 * h + 128)
-            own_stat[g, 2 * i + h : 2 * i + h + 1, :] = log_total[:, here]
-            own_stat[g, 4 + 2 * i + h : 5 + 2 * i + h, :] = delta[:, here]
+            own_stat[g // 2, g % 2, 2 * i + h : 2 * i + h + 1, :] = log_total[:, here]
+            own_stat[g // 2, g % 2, 4 + 2 * i + h : 5 + 2 * i + h, :] = delta[:, here]
 
     def second_pass(g, i):
         at = pair_lanes(g * PER + i)
@@ -469,9 +474,9 @@
         lows, grads = [], []
         for h in range(2):
             here = slice(128 * h, 128 * h + 128)
-            probs = jnp.exp(scores[here] + near - halo_stat[g, 2 * i + h : 2 * i + h + 1, :])
+            probs = jnp.exp(scores[here] + near - halo_stat[g % 2, 2 * i + h : 2 * i + h + 1, :])
             lows.append(probs.astype(BF16))
-            change = prob_grad[here] - halo_stat[g, 4 + 2 * i + h : 5 + 2 * i + h, :]
+            change = prob_grad[here] - halo_stat[g % 2, 4 + 2 * i + h : 5 + 2 * i + h, :]
             grads.append((probs * change).astype(BF16))
         value_part = nn(jnp.concatenate(lows, axis=0), upstream)
         key_part = nn(jnp.concatenate(grads, axis=0), queries)
@@ -495,9 +500,9 @@
 
         arrive(0, g)
         pairs_of(g, first_pass)
-        tell(g)
-
-        @pl.when(jnp.logical_not(late) & (g >= AHEAD - 1) & (g < GROUPS - 1))
+        pl.when(g % 2 == 1)(lambda: tell(g // 2))
+
+        @pl.when(jnp.logical_not(late) & (g >= AHEAD - 1) & (g < jnp.where(turn == 7, GROUPS - 2, GROUPS - 1)))
         def _():
             send(lat_copy, True, 1, g + 1)
             send(lat_copy, False, 1, g + 1)
@@ -514,6 +519,11 @@
     ]
     for store in stores:
         store.start()
+
+    @pl.when(turn == 7)
+    def _():
+        send(lat_copy, True, 1, GROUPS - 1)
+        send(lat_copy, False, 1, GROUPS - 1)
 
     @pl.when(jnp.logical_not(late))
     def _():
@@ -532,7 +542,7 @@
         ]
 
     def second_group(g):
-        hear(g)
+        pl.when(g % 2 == 0)(lambda: hear(g // 2))
         arrive(1, g)
         pairs_of(g, second_pass)
         for copy in finals(g):
@@ -551,7 +561,7 @@
         outer_copy(ph).wait_send()
         each_group(lambda g: inner_copy(ph, g).wait_send())
     for i in range(8):
-        maybe(goes[i], lambda i=i: each_group(lambda g: stat_copy(i, g).wait_send()))
+        maybe(goes[i], lambda i=i: each_group(lambda g: stat_copy(i, g).wait_send(), 0, TOLD))
     for store in stores:
         store.wait()
 
@@ -579,10 +589,10 @@
             pltpu.VMEM((4, 128, 1024), BF16),
             pltpu.VMEM((SLOTS, 128), F32),
             pltpu.VMEM((128, HALO), F32),
-            pltpu.VMEM((GROUPS, 8, 128), F32),
-            pltpu.VMEM((GROUPS, 6, 8, 128), F32),
-            pltpu.VMEM((GROUPS, 8, 8, 128), F32),
-            pltpu.VMEM((GROUPS, 8, HALO), F32),
+            pltpu.VMEM((TOLD, 2, 8, 128), F32),
+            pltpu.VMEM((TOLD, 6, 16, 128), F32),
+            pltpu.VMEM((TOLD, 8, 16, 128), F32),
+            pltpu.VMEM((2, 8, HALO), F32),
             pltpu.VMEM((128, 1024), BF16),
             pltpu.VMEM((128, 1024), BF16),
             pltpu.VMEM((128, 1024), BF16),
@@ -606,8 +616,8 @@
             dma((2, 2, GROUPS)),
             dma((2, GROUPS)),
             dma((2, GROUPS)),
-            dma((8, GROUPS)),
-            dma((8, GROUPS)),
+            dma((8, TOLD)),
+            dma((8, TOLD)),
         ],
         compiler_params=pltpu.CompilerParams(
             collective_id=0, has_side_effects=True, vmem_limit_bytes=48 << 20

time: 47.4 us -> 45.7 us (0.964)
  the two profiles are of different devices: /device:TPU:8 before, /device:TPU:64 now
where the time goes in v4:
time: 45.7 us; the launch traced here: 45.5 us
  Pallas kernels  43.9 us (96%)
  local copies, waits for them, and re-layouts  0.98 us (2%)
  between operations  0.64 us (1%)
    pallas_call x1, Pallas kernels, body(): pl.pallas_call(functools.partial(kernel, lats, lons), out_shape=jax.Shape...  43.9 us
    slice x1, local copies, waits for them, and re-layouts, body(): return tuple((outs[i].reshape(8, 16, 1024) for i in range(4)))  0.98 us

profile of v4, /device:TPU:64, one launch (start us, length us, event | category | flops | bytes accessed | tf_op | source)
XLA Modules:
  0.0 45.5 jit_solution(12266576370522315568)
XLA Ops:
  0.6 43.9 %shard_map.75 = bf16[4,128,1024]{2,1,0:T(8,128)(2,1)S(1)} custom-call(bf16[128,1024]{1,0:T(8,128)(2,1)} %bitcast.8, bf16[128,1024]{1,0:T(8,128)(2,1)} %bitcast.9, bf16[128,1024]{1,0:T(8,128)(2,1)} %bitcast.10, bf16[128,1024]{1,0:T(8,128)(2,1)} %bitcast.11), custom_call_target="tpu_custom_call" | custom-call | tf_op jit(solution)/shard_map/pallas_call | solution.py:581
  44.5 1.0 %fusion = (bf16[1,128,1024]{2,1,0:T(8,128)(2,1)}, bf16[1,128,1024]{2,1,0:T(8,128)(2,1)}, bf16[1,128,1024]{2,1,0:T(8,128)(2,1)}, bf16[1,128,1024]{2,1,0:T(8,128)(2,1)}) fusion(bf16[4,128,1024]{2,1,0:T(8,128)(2,1)S(1)} %shard_map.75), kind=kLoop, calls=%fused_computation | loop fusion | bytes 2097152 | tf_op jit(solution)/shard_map/slice | solution.py:626

commit v5 on v4

--- a/solution.py
+++ b/solution.py
@@ -14,11 +14,12 @@
 F32 = jnp.float32
 
 OWN, NORTH, SOUTH, OUTER, OUTER_N, OUTER_S, INNER, SLOTS = 0, 128, 224, 320, 368, 416, 464, 592
+SIDE = INNER - OUTER
+PADDED = INNER + SIDE
 HALO = SLOTS - NORTH
 GROUPS = 4
 PER = 2
 TOLD = 2
-CHUNK = 208
 AHEAD = 2
 NEG = -1e30
 
@@ -103,6 +104,7 @@
         buf[:, SOUTH:OUTER, :] = jnp.zeros((4, OUTER - SOUTH, 1024), BF16)
         buf[:, OUTER_S:INNER, :] = jnp.zeros((4, 48, 1024), BF16)
 
+    buf[0:2, SLOTS:PADDED, :] = jnp.zeros((2, PADDED - SLOTS, 1024), BF16)
     recv_stat[...] = jnp.zeros(recv_stat.shape, F32)
 
     barrier = pltpu.get_barrier_semaphore()
@@ -333,7 +335,10 @@
             ok = ok & (row + first_row >= 0) & (row + first_row < 8 * lats)
         return jnp.where(ok, 0.0, NEG)
 
-    bias1[...] = bias((SLOTS, 128), 0, 0, 0)
+    bias1[0:OUTER] = bias((OUTER, 128), 0, 0, 0)
+    bias1[OUTER:INNER] = jnp.maximum(
+        bias((SIDE, 128), 0, OUTER, 0), bias((SIDE, 128), 0, INNER, 0)
+    )
     bias2[...] = bias((128, HALO), 0, 0, NORTH)
 
     patch = lax.broadcasted_iota(jnp.int32, (128, 128), 0)
@@ -414,6 +419,15 @@
     high = jnp.where(lane < HD, 0.0, 1.0).astype(BF16)
     low_f, high_f = low.astype(F32), high.astype(F32)
 
+    def column_mask(shape, axis, edge):
+        col = lax.broadcasted_iota(jnp.int32, shape, axis) & 15
+        return jnp.where((col >= edge) & (col < edge + REACH), 1.0, 0.0).astype(BF16)
+
+    near_outer = column_mask((256, 128), 0, outer_first)
+    near_inner = column_mask((256, 128), 0, inner_first)
+    lanes_outer = column_mask((SIDE, 256), 1, outer_first)
+    lanes_inner = column_mask((SIDE, 256), 1, inner_first)
+
     def split(x):
         return jnp.concatenate((x * low, x * high), axis=0)
 
@@ -428,11 +442,18 @@
         keys, values = buf[0, :, at], buf[1, :, at]
         queries = split(buf[2, OWN:NORTH, at] * jnp.asarray(0.125, BF16))
         upstream = split(buf[3, OWN:NORTH, at])
-        cuts = [(r, min(r + CHUNK, SLOTS)) for r in range(0, SLOTS, CHUNK)]
+
+        def product(x, lo, hi, y):
+            if lo < OUTER:
+                return nt(x[lo:hi], y)
+            both = jnp.concatenate((x[OUTER:INNER], x[INNER:PADDED]), axis=1)
+            return nt(both, jnp.concatenate((y * near_outer, y * near_inner), axis=1))
+
+        cuts = [(0, 160), (160, OUTER), (OUTER, INNER)]
         peak = jnp.full((8, 256), NEG, F32)
         for lo, hi in cuts:
             near = bias1[lo:hi]
-            part = nt(keys[lo:hi], queries) + jnp.concatenate((near, near), axis=1)
+            part = product(keys, lo, hi, queries) + jnp.concatenate((near, near), axis=1)
             work[lo:hi] = part
             peak = jnp.maximum(peak, jnp.max(part.reshape(-1, 8, 256), axis=0))
         peak = jnp.max(peak, axis=0, keepdims=True)
@@ -440,7 +461,7 @@
         delta = jnp.zeros((8, 256), F32)
         for lo, hi in cuts:
             e = jnp.exp(work[lo:hi] - peak)
-            part = nt(values[lo:hi], upstream)
+            part = product(values, lo, hi, upstream)
             work[lo:hi] = e
             work2[lo:hi] = part
             total = total + jnp.sum(e.reshape(-1, 8, 256), axis=0)
@@ -450,8 +471,16 @@
         delta = jnp.sum(delta, axis=0, keepdims=True) * scale
         for lo, hi in cuts:
             probs = work[lo:hi] * scale
-            low_probs[lo:hi] = probs.astype(BF16)
-            low_grads[lo:hi] = (probs * (work2[lo:hi] - delta)).astype(BF16)
+            probs_bf = probs.astype(BF16)
+            grads_bf = (probs * (work2[lo:hi] - delta)).astype(BF16)
+            if lo < OUTER:
+                low_probs[lo:hi] = probs_bf
+                low_grads[lo:hi] = grads_bf
+            else:
+                low_probs[lo:hi] = probs_bf * lanes_outer
+                low_grads[lo:hi] = grads_bf * lanes_outer
+                low_probs[INNER:PADDED] = probs_bf * lanes_inner
+                low_grads[INNER:PADDED] = grads_bf * lanes_inner
         probs_low, score_grad = low_probs[...], low_grads[...]
         att[:, at] = joined(tn(values, probs_low)).astype(BF16)
         dq[:, at] = (joined(tn(keys, score_grad)) * 0.125).astype(BF16)
@@ -584,10 +613,10 @@
         in_specs=[pl.BlockSpec(memory_space=pltpu.HBM)] * 4,
         out_specs=pl.BlockSpec(memory_space=pl.ANY),
         scratch_shapes=[
-            pltpu.VMEM((4, SLOTS, 1024), BF16),
+            pltpu.VMEM((4, PADDED, 1024), BF16),
             pltpu.VMEM((4, 48, 1024), BF16),
             pltpu.VMEM((4, 128, 1024), BF16),
-            pltpu.VMEM((SLOTS, 128), F32),
+            pltpu.VMEM((INNER, 128), F32),
             pltpu.VMEM((128, HALO), F32),
             pltpu.VMEM((TOLD, 2, 8, 128), F32),
             pltpu.VMEM((TOLD, 6, 16, 128), F32),
@@ -599,10 +628,10 @@
             pltpu.VMEM((128, 1024), BF16),
             pltpu.VMEM((128, 1024), F32),
             pltpu.VMEM((128, 1024), F32),
-            pltpu.VMEM((SLOTS, 256), F32),
-            pltpu.VMEM((SLOTS, 256), F32),
-            pltpu.VMEM((SLOTS, 256), BF16),
-            pltpu.VMEM((SLOTS, 256), BF16),
+            pltpu.VMEM((INNER, 256), F32),
+            pltpu.VMEM((INNER, 256), F32),
+            pltpu.VMEM((PADDED, 256), BF16),
+            pltpu.VMEM((PADDED, 256), BF16),
             pltpu.VMEM((5, 128, 128), BF16),
             pltpu.SemaphoreType.REGULAR,
             dma((4,)),

time: 45.7 us -> 45.4 us (level)
  no operation moved by 1% of the time
where the time goes in v5:
time: 45.4 us; the launch traced here: 45.2 us
  Pallas kernels  43.6 us (96%)
  local copies, waits for them, and re-layouts  0.98 us (2%)
  between operations  0.64 us (1%)
    pallas_call x1, Pallas kernels, body(): pl.pallas_call(functools.partial(kernel, lats, lons), out_shape=jax.Shape...  43.6 us
    slice x1, local copies, waits for them, and re-layouts, body(): return tuple((outs[i].reshape(8, 16, 1024) for i in range(4)))  0.98 us

profile of v5, /device:TPU:64, one launch (start us, length us, event | category | flops | bytes accessed | tf_op | source)
XLA Modules:
  0.0 45.2 jit_solution(437655877357976423)
XLA Ops:
  0.6 43.6 %shard_map.75 = bf16[4,128,1024]{2,1,0:T(8,128)(2,1)S(1)} custom-call(bf16[128,1024]{1,0:T(8,128)(2,1)} %bitcast.8, bf16[128,1024]{1,0:T(8,128)(2,1)} %bitcast.9, bf16[128,1024]{1,0:T(8,128)(2,1)} %bitcast.10, bf16[128,1024]{1,0:T(8,128)(2,1)} %bitcast.11), custom_call_target="tpu_custom_call" | custom-call | tf_op jit(solution)/shard_map/pallas_call | solution.py:610
  44.2 1.0 %fusion = (bf16[1,128,1024]{2,1,0:T(8,128)(2,1)}, bf16[1,128,1024]{2,1,0:T(8,128)(2,1)}, bf16[1,128,1024]{2,1,0:T(8,128)(2,1)}, bf16[1,128,1024]{2,1,0:T(8,128)(2,1)}) fusion(bf16[4,128,1024]{2,1,0:T(8,128)(2,1)S(1)} %shard_map.75), kind=kLoop, calls=%fused_computation | loop fusion | bytes 2097152 | tf_op jit(solution)/shard_map/slice | solution.py:655
